TPU v7x, 32 devices: a whole 2x2x4 slice. The times are simulated.
32 devices in a mesh: batch: 4 (over z), seq: 8 (over y, x, core).
Axes of the slice: x: 2, y: 2, z: 4, core: 2. Of those that a mesh axis runs over, the one named last changes fastest.
Arguments:
- latents: bfloat16 [4, 1024, 1024], P('batch', 'seq'), may hold values from -6 to 6
- pixels: bfloat16 [4, 3, 16384], P('batch', None, 'seq'), may hold values from -4 to 4
- counts: int32 [4, 33], P('batch'), may hold values from 1 to 1024, 16384 in all within a row
- latent_image: int32 [4, 1024], P('batch'), may hold values from 0 to 32, as said below
- query_gain: float32 [1024], replicated, may hold values from 0.5 to 1.5
- query_shift: float32 [1024], replicated, may hold values from -3 to 3
- query_weight: bfloat16 [1024, 1024], replicated, may hold values from -0.1875 to 0.1875
- input_gain: float32 [261], replicated, may hold values from 0.5 to 1.5
- input_shift: float32 [261], replicated, may hold values from -3 to 3
- kv_weight: bfloat16 [261, 2048], replicated, may hold values from -0.375 to 0.375
- out_weight: bfloat16 [1024, 1024], replicated, may hold values from -1.5 to 1.5
- mlp_gain: float32 [1024], replicated, may hold values from 0.5 to 1.5
- mlp_shift: float32 [1024], replicated, may hold values from -3 to 3
- up_weight: bfloat16 [1024, 1024], replicated, may hold values from -0.1875 to 0.1875
- down_weight: bfloat16 [1024, 1024], replicated, may hold values from -0.25 to 0.25
- cotangent: bfloat16 [4, 1024, 1024], P('batch', 'seq'), may hold values from -6 to 6
Outputs:
- mixed: bfloat16 [4, 1024, 1024], P('batch', 'seq')
- latent_grad: float32 [4, 1024, 1024], P('batch', 'seq')
- pixel_grad: float32 [4, 3, 16384], P('batch', None, 'seq')
- query_gain_grad: float32 [1024], P(('batch', 'seq'))
- query_shift_grad: float32 [1024], P(('batch', 'seq'))
- query_weight_grad: float32 [1024, 1024], P(('batch', 'seq'))
- input_gain_grad: float32 [261], replicated
- input_shift_grad: float32 [261], replicated
- kv_weight_grad: float32 [261, 2048], P(None, ('batch', 'seq'))
- out_weight_grad: float32 [1024, 1024], P(('batch', 'seq'))
- mlp_gain_grad: float32 [1024], P(('batch', 'seq'))
- mlp_shift_grad: float32 [1024], P(('batch', 'seq'))
- up_weight_grad: float32 [1024, 1024], P(('batch', 'seq'))
- down_weight_grad: float32 [1024, 1024], P(('batch', 'seq'))
Inputs may be any that keep to these rules, and one draw needn't show every extreme that they name: The 33 counts of a packed row sum to 16384; images lie one after another in the row in the order of counts. `latent_image`: each latent may read any image of its packed row, in no particular order; every image has at least one latent.
All inputs are finite; a program needn't handle non-finite values.
Results may differ from a plain program's by a relative error of at most 0.015.
Values may be sent and summed in bfloat16 or wider, within the bound.
A program may use at most 256 MiB of HBM per device.

v0:
```python
import math

import jax
import jax.numpy as jnp
from jax import lax
from jax.sharding import PartitionSpec as P

BANDS = 64
IMG_W = 32


top_freq = 112.0
tiny = 1e-05
floor_value = -1e30


def norm_rows(values, gain_vec, shift_vec):
    center = values - jnp.mean(values, axis=-1, keepdims=True)
    spread = jnp.mean(center * center, axis=-1, keepdims=True)
    return center * lax.rsqrt(spread + tiny) * gain_vec + shift_vec


def gelu_exact(values):
    return jax.nn.gelu(values, approximate=False)


def features(colors, in_image):
    row_pos = (in_image // IMG_W).astype(jnp.float32)
    col_pos = (in_image % IMG_W).astype(jnp.float32)
    y_coord = 2.0 * row_pos / (IMG_W - 1) - 1.0
    x_coord = 2.0 * col_pos / (IMG_W - 1) - 1.0
    bands_vec = jnp.linspace(1.0, top_freq, BANDS).astype(jnp.float32)
    y_phase = math.pi * y_coord[:, None] * bands_vec[None, :]
    x_phase = math.pi * x_coord[:, None] * bands_vec[None, :]
    return jnp.concatenate(
        [
            colors,
            y_coord[:, None],
            x_coord[:, None],
            jnp.sin(y_phase),
            jnp.sin(x_phase),
            jnp.cos(y_phase),
            jnp.cos(x_phase),
        ],
        axis=1,
    )


def image_of(places, lengths):
    ends = jnp.cumsum(lengths)
    image_ids = jnp.sum((places[:, None] >= ends[None, :]).astype(jnp.int32), axis=1)
    starts = ends - lengths
    number = jnp.arange(lengths.shape[0], dtype=jnp.int32)
    firsts = jnp.sum(jnp.where(image_ids[:, None] == number[None, :], starts[None, :], 0), axis=1)
    return (image_ids, places - firsts)


def matmul(operand, factor):
    return jnp.dot(operand, factor, preferred_element_type=jnp.float32)


def contract_rows(operand, factor):
    return lax.dot_general(
        operand, factor, (((0,), (0,)), ((), ())), preferred_element_type=jnp.float32
    )


def contract_cols(operand, factor):
    return lax.dot_general(
        operand, factor, (((1,), (1,)), ((), ())), preferred_element_type=jnp.float32
    )


def body(
    latents,
    pixels,
    counts,
    latent_image,
    query_gain,
    query_shift,
    query_weight,
    input_gain,
    input_shift,
    kv_weight,
    out_weight,
    mlp_gain,
    mlp_shift,
    up_weight,
    down_weight,
    cotangent,
):
    width = query_weight.shape[0]
    pix_dev = pixels.shape[2]
    score_scale = width ** (-0.5)
    seq_rank = lax.axis_index("seq")
    places = seq_rank * pix_dev + jnp.arange(pix_dev, dtype=jnp.int32)
    image_ids, in_image = image_of(places, counts[0])
    inputs = features(pixels[0].astype(jnp.float32).T, in_image)
    normed_in, input_back = jax.vjp(norm_rows, inputs, input_gain, input_shift)
    normed_in = normed_in.astype(jnp.bfloat16)
    key_value = matmul(normed_in, kv_weight).astype(jnp.bfloat16)
    key_rows = key_value[:, :width]
    value_rows = key_value[:, width:]
    latent_in = latents[0].astype(jnp.float32)
    normed_lat, query_back = jax.vjp(norm_rows, latent_in, query_gain, query_shift)
    normed_lat = normed_lat.astype(jnp.bfloat16)
    queries = matmul(normed_lat, query_weight).astype(jnp.bfloat16)
    all_queries = lax.all_gather(queries, "seq", axis=0, tiled=True)
    scores = contract_cols(all_queries, key_rows) * score_scale
    same_image = latent_image[0][:, None] == image_ids[None, :]
    masked = jnp.where(same_image, scores, floor_value)
    local_top = jnp.max(masked, axis=1)
    local_total = jnp.sum(jnp.where(same_image, jnp.exp(masked - local_top[:, None]), 0.0), axis=1)
    row_top = lax.pmax(local_top, "seq")
    row_total = lax.psum(local_total * jnp.exp(local_top - row_top), "seq")
    log_total = row_top + jnp.log(row_total)
    probs = jnp.exp(jnp.where(same_image, scores - log_total[:, None], floor_value))
    probs_low = probs.astype(jnp.bfloat16)
    attended = lax.psum_scatter(
        matmul(probs_low, value_rows), "seq", scatter_dimension=0, tiled=True
    )
    merged = attended.astype(jnp.bfloat16)
    residual_mid = latent_in + matmul(merged, out_weight)
    normed_mid, mlp_back = jax.vjp(norm_rows, residual_mid, mlp_gain, mlp_shift)
    normed_mid = normed_mid.astype(jnp.bfloat16)
    hidden_pre = matmul(normed_mid, up_weight)
    hidden_act, gelu_back = jax.vjp(gelu_exact, hidden_pre)
    hidden_low = hidden_act.astype(jnp.bfloat16)
    mixed = (residual_mid + matmul(hidden_low, down_weight)).astype(jnp.bfloat16)
    out_grad = cotangent[0]
    down_grad = contract_rows(hidden_low, out_grad)
    act_grad = contract_cols(out_grad, down_weight)
    pre_grad = gelu_back(act_grad)[0].astype(jnp.bfloat16)
    up_grad = contract_rows(normed_mid, pre_grad)
    mid_norm_grad = contract_cols(pre_grad, up_weight)
    mid_ln_grad, mlp_gain_grad, mlp_shift_grad = mlp_back(mid_norm_grad)
    mid_grad = out_grad.astype(jnp.float32) + mid_ln_grad
    branch_grad = mid_grad.astype(jnp.bfloat16)
    out_weight_grad = contract_rows(merged, branch_grad)
    att_grad = contract_cols(branch_grad, out_weight).astype(jnp.bfloat16)
    all_att_grads = lax.all_gather(att_grad, "seq", axis=0, tiled=True)
    prob_grad = contract_cols(all_att_grads, value_rows)
    delta_part = jnp.sum(probs * prob_grad, axis=1)
    delta_all = lax.psum(delta_part, "seq")
    score_grad = (probs * (prob_grad - delta_all[:, None])).astype(jnp.bfloat16)
    back_queries = lax.all_gather(queries, "seq", axis=0, tiled=True)
    query_grad = lax.psum_scatter(
        (matmul(score_grad, key_rows) * score_scale).astype(jnp.bfloat16),
        "seq",
        scatter_dimension=0,
        tiled=True,
    )
    key_grad = contract_rows(score_grad, back_queries) * score_scale
    value_grad = contract_rows(probs_low, all_att_grads)
    kv_grad = jnp.concatenate([key_grad, value_grad], axis=1).astype(jnp.bfloat16)
    kv_weight_grad = contract_rows(normed_in, kv_grad)
    in_norm_grad = contract_cols(kv_grad, kv_weight)
    inputs_grad, input_gain_grad, input_shift_grad = input_back(in_norm_grad)
    pixel_grad = inputs_grad[:, :3].T[None]
    query_weight_grad = contract_rows(normed_lat, query_grad)
    lat_norm_grad = contract_cols(query_grad, query_weight)
    lat_ln_grad, query_gain_grad, query_shift_grad = query_back(lat_norm_grad)
    latent_grad = (mid_grad + lat_ln_grad)[None]
    reduced = (
        lax.psum_scatter(query_gain_grad, ("batch", "seq"), scatter_dimension=0, tiled=True),
        lax.psum_scatter(query_shift_grad, ("batch", "seq"), scatter_dimension=0, tiled=True),
        lax.psum_scatter(query_weight_grad, ("batch", "seq"), scatter_dimension=0, tiled=True),
        lax.psum_scatter(kv_weight_grad, ("batch", "seq"), scatter_dimension=1, tiled=True),
        lax.psum_scatter(out_weight_grad, ("batch", "seq"), scatter_dimension=0, tiled=True),
        lax.psum_scatter(mlp_gain_grad, ("batch", "seq"), scatter_dimension=0, tiled=True),
        lax.psum_scatter(mlp_shift_grad, ("batch", "seq"), scatter_dimension=0, tiled=True),
        lax.psum_scatter(up_grad, ("batch", "seq"), scatter_dimension=0, tiled=True),
        lax.psum_scatter(down_grad, ("batch", "seq"), scatter_dimension=0, tiled=True),
    )
    feature_sums = lax.psum((input_gain_grad, input_shift_grad), ("batch", "seq"))
    return (
        mixed[None],
        latent_grad,
        pixel_grad,
        reduced[0],
        reduced[1],
        reduced[2],
        feature_sums[0],
        feature_sums[1],
        reduced[3],
        reduced[4],
        reduced[5],
        reduced[6],
        reduced[7],
        reduced[8],
    )


def solution(mesh):
    return jax.shard_map(
        body,
        mesh=mesh,
        in_specs=(
            P("batch", "seq", None),
            P("batch", None, "seq"),
            P("batch", None),
            P("batch", None),
            P(),
            P(),
            P(),
            P(),
            P(),
            P(),
            P(),
            P(),
            P(),
            P(),
            P(),
            P("batch", "seq", None),
        ),
        out_specs=(
            P("batch", "seq", None),
            P("batch", "seq", None),
            P("batch", None, "seq"),
            P(("batch", "seq")),
            P(("batch", "seq")),
            P(("batch", "seq"), None),
            P(),
            P(),
            P(None, ("batch", "seq")),
            P(("batch", "seq"), None),
            P(("batch", "seq")),
            P(("batch", "seq")),
            P(("batch", "seq"), None),
            P(("batch", "seq"), None),
        ),
        check_vma=False,
    )
```

profile of v0, /device:TPU:0, one launch (start us, length us, event | category | flops | bytes accessed | tf_op | source)
XLA Modules:
  0.0 943.6 jit_solution(679830518746716186)
XLA Ops:
  7.2 1.2 convert_reduce_fusion
  8.5 1.2 fusion.29
  9.6 2.9 convolution_convert_fusion.3
  12.7 0.8 copy.36
  13.5 0.1 reduce.10
  13.6 0.1 convert_reduce_fusion.1
  13.8 0.7 fusion.66
  14.5 0.1 select_reduce_fusion
  14.6 4.9 fusion.44
  19.6 11.4 %concatenate.12 = f32[2048,261]{0,1:T(8,128)} concatenate(f32[2048,3]{0,1:T(4,128)S(1)} %convert_bitcast_fusion.1, f32[2048,1]{0,1:T(1,128)S(1)} %multiply_add_fusion.1, f32[2048,1]{0,1:T(1,128)S(1)} %get-tuple-element.96, f32[2048,64]{0,1:T(8,128)} %get-tuple-element.101, f32[2048,64]{0,1:T(8,128)S(1)} %get-tuple-element.98, f32[2048,64]{0,1:T(8,128)} %get-tuple-element.100, ...), dimensions={1} | concatenate | bytes 4276224 | tf_op jit(solution)/shard_map/concatenate | solution.py:35
  31.1 1.9 multiply_reduce_fusion.3
  33.0 10.2 %convolution_convert_fusion = bf16[2048,2048]{1,0:T(8,128)(2,1)} fusion(bf16[261,2048]{1,0:T(8,128)(2,1)} %param.25, f32[2048,261]{0,1:T(8,128)} %concatenate.12, f32[261]{0:T(512)S(1)} %copy-done.27, f32[261]{0:T(512)S(1)} %copy-done.23, f32[2048]{0:T(1024)S(1)} %fusion.62, f32[2048]{0:T(1024)S(1)} %add_multiply_fusion), kind=kOutput, calls=%fused_computation.9 | convolution fusion | flops 2196293632 | bytes 11614248 | tf_op jit(solution)/shard_map/dot_general | solution.py:59
  43.1 0.2 all-gather.3.cloned.1.call-done
  43.3 10.7 %fusion.2 = (f32[1024]{0:T(1024)S(1)}, f32[1024,2048]{1,0:T(8,128)}) fusion(s32[2048]{0:T(1024)S(1)} %convert_reduce_fusion.1, s32[1024]{0:T(1024)S(1)} %bitcast.90, bf16[1024,1024]{1,0:T(8,128)(2,1)} %all-gather.3.cloned.1.call-done, bf16[2048,2048]{1,0:T(8,128)(2,1)} %convolution_convert_fusion), kind=kOutput, calls=%fused_computation.10 | convolution fusion | flops 4303354880 | bytes 14696448 | tf_op jit(solution)/shard_map/dot_general | solution.py:69
  54.1 14.8 %pmax.7 = f32[1024]{0:T(1024)S(1)} all-reduce(f32[1024]{0:T(1024)S(1)} %get-tuple-element.104), channel_id=1, replica_groups=mesh['batch'=4,'seq'=8] {'seq'}, use_global_device_ids=true, to_apply=%region_12.13 | all-reduce | flops 1024 | bytes 8192 | tf_op jit(solution)/shard_map/pmax | solution.py:114
  68.9 4.8 fusion
  73.7 11.8 %psum.28 = f32[1024]{0:T(1024)S(1)} all-reduce(f32[1024]{0:T(1024)S(1)} %exponential_multiply_fusion), channel_id=1, replica_groups=mesh['batch'=4,'seq'=8] {'seq'}, use_global_device_ids=true, to_apply=%region_14.15 | all-reduce | flops 1024 | bytes 8192 | tf_op jit(solution)/shard_map/psum | solution.py:115
  85.5 11.1 %fusion.7 = f32[1024,1024]{1,0:T(8,128)} fusion(bf16[2048,2048]{1,0:T(8,128)(2,1)} %convolution_convert_fusion, f32[1024,2048]{1,0:T(8,128)} %get-tuple-element.105, f32[1024]{0:T(1024)S(1)} %log_add_fusion, s32[2048]{0:T(1024)S(1)} %convert_reduce_fusion.1, s32[1024]{0:T(1024)S(1)} %bitcast.92), kind=kOutput, calls=%fused_computation.17 | convolution fusion | flops 4305453056 | bytes 16793600 | tf_op jit(solution)/shard_map/dot_general | solution.py:59
  96.6 50.8 %reduce-scatter.8.cloned.1.call-done = f32[128,1024]{1,0:T(8,128)} async-done(((f32[1024,1024]{1,0:T(8,128)}), f32[128,1024]{1,0:T(8,128)}) %reduce-scatter.8.cloned.1.call-update) | async-done | bytes 524304 | tf_op jit(solution)/shard_map/reduce_scatter | solution.py:119
  147.4 2.4 fusion.82
  149.9 0.2 multiply_reduce_fusion.6
  150.1 0.5 fusion.76
  150.6 0.8 copy-done.15
  151.4 1.9 add_convert_fusion.1
  153.3 1.0 multiply_reduce_fusion.4
  154.3 0.3 fusion.81
  154.6 0.1 fusion.37
  154.8 0.3 copy-done.5
  155.1 1.6 convolution_convert_fusion.2
  156.7 28.0 %all-gather.5.cloned.1.call-done = bf16[1024,1024]{1,0:T(8,128)(2,1)} async-done(((bf16[128,1024]{1,0:T(8,128)(2,1)}), bf16[1024,1024]{1,0:T(8,128)(2,1)}) %all-gather.5.cloned.1.call-update) | async-done | bytes 2097168 | tf_op jit(solution)/shard_map/all_gather | solution.py:141
  184.7 11.4 %multiply_reduce_fusion = (f32[1024]{0:T(1024)S(1)}, f32[1024,2048]{1,0:T(8,128)}) fusion(f32[1024]{0:T(1024)S(1)} %log_add_fusion, f32[1024,2048]{1,0:T(8,128)} %get-tuple-element.105, s32[2048]{0:T(1024)S(1)} %convert_reduce_fusion.1, s32[1024]{0:T(1024)S(1)} %bitcast.93, bf16[1024,1024]{1,0:T(8,128)(2,1)} %all-gather.5.cloned.1.call-done, ...), kind=kOutput, calls=%fused_computation.8 | convolution fusion | flops 4307549184 | bytes 23089152 | tf_op jit(solution)/shard_map/dot_general | solution.py:69
  196.1 13.1 %psum.29 = f32[1024]{0:T(1024)S(1)} all-reduce(f32[1024]{0:T(1024)S(1)} %get-tuple-element.109), channel_id=1, replica_groups=mesh['batch'=4,'seq'=8] {'seq'}, use_global_device_ids=true, to_apply=%region_21.22 | all-reduce | flops 1024 | bytes 8192 | tf_op jit(solution)/shard_map/psum | solution.py:144
  209.2 7.2 multiply_convert_fusion.1
  216.4 1.9 copy-done.6
  218.3 8.0 multiply_convert_fusion.2
  226.3 8.8 reduce-scatter.14.cloned.1.call-start
  235.1 7.9 multiply_convert_fusion
  243.0 10.5 %convolution_convert_fusion.1 = bf16[2048,1024]{0,1:T(8,128)(2,1)S(1)} fusion(bf16[1024,1024]{1,0:T(8,128)(2,1)S(1)} %copy-done.25, f32[1024,2048]{1,0:T(8,128)} %get-tuple-element.105, f32[1024]{0:T(1024)S(1)} %log_add_fusion, s32[2048]{0:T(1024)S(1)} %convert_reduce_fusion.1, s32[1024]{0:T(1024)S(1)} %bitcast.95), kind=kOutput, calls=%fused_computation.14 | convolution fusion | flops 4307550208 | bytes 14696448 | tf_op jit(solution)/shard_map/dot_general | solution.py:63
  253.5 1.9 copy-done.30
  255.4 6.8 fusion.3
  262.3 2.7 fusion.48
  265.1 2.8 fusion.75
  268.0 3.6 fusion.38
  271.8 0.6 copy-done.19
  272.4 3.8 fusion.71
  276.2 3.9 fusion.18
  280.1 1.3 copy-done.31
  281.4 2.9 multiply_reduce_fusion.1
  284.4 0.6 fusion.80
  285.0 0.6 copy.37
  285.6 0.3 copy-done.7
  286.0 0.9 fusion.79
  286.9 0.3 fusion.28
  287.3 39.4 %all-reduce.4 = (f32[1024]{0:T(1024)S(1)}, f32[1024]{0:T(1024)S(1)}, f32[261]{0:T(512)}, f32[261]{0:T(512)}, f32[1024]{0:T(1024)S(1)}, /*index=5*/f32[1024]{0:T(1024)S(1)}) all-reduce(f32[1024]{0:T(1024)S(1)} %get-tuple-element.75, f32[1024]{0:T(1024)S(1)} %get-tuple-element.78, ...), channel_id=4, replica_groups=mesh['batch'=4,'seq'=8] {'batch','seq'}, use_global_device_ids=true, to_apply=%region_28.29.clone | all-reduce | flops 4618 | bytes 36944
  326.7 0.6 dynamic-slice
  327.2 0.6 dynamic-slice.1
  327.8 0.6 dynamic-slice.2
  328.4 0.6 dynamic-slice.3
  329.0 2.0 add_bitcast_fusion
  331.0 44.5 %reduce-scatter.14.cloned.1.call-done = f32[261,64]{0,1:T(8,128)} async-done(((f32[261,2048]{0,1:T(8,128)}), f32[261,64]{0,1:T(8,128)}) %reduce-scatter.14.cloned.1.call-update) | async-done | bytes 66832 | tf_op jit(solution)/shard_map/reduce_scatter | solution.py:168
  375.5 142.5 %reduce-scatter.16.cloned.1.call-done = f32[32,1024]{1,0:T(8,128)} async-done(((f32[1024,1024]{1,0:T(8,128)}), f32[32,1024]{1,0:T(8,128)}) %reduce-scatter.16.cloned.1.call-update) | async-done | bytes 131088 | tf_op jit(solution)/shard_map/reduce_scatter | solution.py:169
  518.0 139.5 %reduce-scatter.18.cloned.1.call-done = f32[32,1024]{1,0:T(8,128)} async-done(((f32[1024,1024]{1,0:T(8,128)}), f32[32,1024]{1,0:T(8,128)}) %reduce-scatter.18.cloned.1.call-update) | async-done | bytes 131088 | tf_op jit(solution)/shard_map/reduce_scatter | solution.py:172
  657.6 139.5 %reduce-scatter.20.cloned.1.call-done = f32[32,1024]{1,0:T(8,128)} async-done(((f32[1024,1024]{1,0:T(8,128)}), f32[32,1024]{1,0:T(8,128)}) %reduce-scatter.20.cloned.1.call-update) | async-done | bytes 131088 | tf_op jit(solution)/shard_map/reduce_scatter | solution.py:173
  797.0 139.7 %reduce-scatter.12.cloned.1.call-done = f32[32,1024]{1,0:T(8,128)} async-done(((f32[1024,1024]{1,0:T(8,128)}), f32[32,1024]{1,0:T(8,128)}) %reduce-scatter.12.cloned.1.call-update) | async-done | bytes 131088 | tf_op jit(solution)/shard_map/reduce_scatter | solution.py:167
  (99 shorter events, 1.1 us)
Async XLA Ops:
  7.2 142.9 %copy-start = (bf16[1024,1024]{1,0:T(8,128)(2,1)S(1)}, bf16[1024,1024]{1,0:T(8,128)(2,1)}, u32[]{:S(2)}) copy-start(bf16[1024,1024]{1,0:T(8,128)(2,1)} %param.29) | copy-start | bytes 6291460
  7.2 12.4 %copy-start.17 = (bf16[1,3,2048]{2,1,0:T(4,128)(2,1)S(1)}, bf16[1,3,2048]{2,1,0:T(4,128)(2,1)}, u32[]{:S(2)}) copy-start(bf16[1,3,2048]{2,1,0:T(4,128)(2,1)} %param.17) | copy-start | bytes 36868
  7.2 36.1 %all-gather.3.cloned.1.call-start = ((), (), s32[]{:S(2)}) async-start(), calls=%async_computation.7 | async-start | bytes 2359296 | tf_op jit(solution)/shard_map/all_gather | solution.py:108
  12.6 134.8 %reduce-scatter.8.cloned.1.call-start = ((), (), s32[]{:S(2)}) async-start(), calls=%async_computation.8 | async-start | bytes 4718592 | tf_op jit(solution)/shard_map/reduce_scatter | solution.py:119
  14.6 18.3 %copy-start.23 = (f32[261]{0:T(512)S(1)}, f32[261]{0:T(512)}, u32[]{:S(2)}) copy-start(f32[261]{0:T(512)} %param.23) | copy-start | bytes 3136
  14.6 18.3 %copy-start.27 = (f32[261]{0:T(512)S(1)}, f32[261]{0:T(512)}, u32[]{:S(2)}) copy-start(f32[261]{0:T(512)} %param.24) | copy-start | bytes 3136
  32.9 10.4 %copy-start.20 = (s32[1,1024]{1,0:T(1,128)S(1)}, s32[1,1024]{1,0:T(1,128)}, u32[]{:S(2)}) copy-start(s32[1,1024]{1,0:T(1,128)} %param.19) | copy-start | bytes 12292
  96.5 50.9 %copy-start.4 = (bf16[1,128,1024]{2,1,0:T(8,128)(2,1)S(1)}, bf16[1,128,1024]{2,1,0:T(8,128)(2,1)}, u32[]{:S(2)}) copy-start(bf16[1,128,1024]{2,1,0:T(8,128)(2,1)} %param.16) | copy-start | bytes 786436
  96.5 53.6 %copy-start.18 = (f32[1024]{0:T(1024)S(1)}, f32[1024]{0:T(1024)}, u32[]{:S(2)}) copy-start(f32[1024]{0:T(1024)} %param.27) | copy-start | bytes 12292
  96.5 53.6 %copy-start.21 = (f32[1024]{0:T(1024)S(1)}, f32[1024]{0:T(1024)}, u32[]{:S(2)}) copy-start(f32[1024]{0:T(1024)} %param.28) | copy-start | bytes 12292
  96.6 54.8 %copy-start.11 = (bf16[1,128,1024]{2,1,0:T(8,128)(2,1)S(1)}, bf16[1,128,1024]{2,1,0:T(8,128)(2,1)}, u32[]{:S(2)}) copy-start(bf16[1,128,1024]{2,1,0:T(8,128)(2,1)} %param.31) | copy-start | bytes 786436
  96.6 88.1 %all-gather.5.cloned.1.call-start = ((), (), s32[]{:S(2)}) async-start(), calls=%async_computation.9 | async-start | bytes 2359296 | tf_op jit(solution)/shard_map/all_gather | solution.py:141
  147.4 4.0 copy-start.24
  150.6 0.8 copy-start.15
  153.3 1.3 copy-start.9
  153.3 1.3 copy-start.12
  153.3 1.8 copy-start.5
  156.6 115.1 %reduce-scatter.10.cloned.1.call-start = ((), (), s32[]{:S(2)}) async-start(), calls=%async_computation.10 | async-start | bytes 2359296 | tf_op jit(solution)/shard_map/reduce_scatter | solution.py:147
  216.4 1.9 copy-start.6
  226.3 149.2 %reduce-scatter.14.cloned.1.call-start = ((), (), s32[]{:S(2)}) async-start(), calls=%async_computation.12 | async-start | bytes 3244032 | tf_op jit(solution)/shard_map/reduce_scatter | solution.py:168
  235.1 7.9 copy-start.25
  243.0 10.5 %copy-start.28 = (bf16[2048,1024]{0,1:T(8,128)(2,1)}, bf16[2048,1024]{0,1:T(8,128)(2,1)S(1)}, u32[]{:S(2)}) copy-start(bf16[2048,1024]{0,1:T(8,128)(2,1)S(1)} %multiply_convert_fusion) | copy-start | bytes 12582916
  243.0 12.4 %copy-start.2 = (f32[2048,261]{0,1:T(8,128)S(1)}, f32[2048,261]{0,1:T(8,128)}, u32[]{:S(2)}) copy-start(f32[2048,261]{0,1:T(8,128)} %concatenate.12) | copy-start | bytes 6414340
  253.5 1.9 copy-start.30
  255.4 6.9 copy-start.8
  262.3 2.9 copy-start.10
  262.3 255.7 %reduce-scatter.16.cloned.1.call-start = ((), (), s32[]{:S(2)}) async-start(), calls=%async_computation.13 | async-start | bytes 4325376 | tf_op jit(solution)/shard_map/reduce_scatter | solution.py:169
  265.1 2.9 copy-start.13
  265.1 2.9 copy-start.16
  265.1 392.5 %reduce-scatter.18.cloned.1.call-start = ((), (), s32[]{:S(2)}) async-start(), calls=%async_computation.14 | async-start | bytes 4325376 | tf_op jit(solution)/shard_map/reduce_scatter | solution.py:172
  268.0 529.1 %reduce-scatter.20.cloned.1.call-start = ((), (), s32[]{:S(2)}) async-start(), calls=%async_computation.15 | async-start | bytes 4325376 | tf_op jit(solution)/shard_map/reduce_scatter | solution.py:173
  271.7 0.7 copy-start.19
  271.7 0.7 copy-start.22
  271.7 665.0 %reduce-scatter.12.cloned.1.call-start = ((), (), s32[]{:S(2)}) async-start(), calls=%async_computation.11 | async-start | bytes 4325376 | tf_op jit(solution)/shard_map/reduce_scatter | solution.py:167
  276.2 4.0 copy-start.3
  276.2 4.0 copy-start.26
  276.2 4.0 copy-start.29
  276.2 5.2 copy-start.31
  284.3 1.6 copy-start.7
  284.3 1.6 copy-start.14
  284.4 652.3 %copy-start.1 = (bf16[1024,1024]{1,0:T(8,128)(2,1)S(1)}, bf16[1024,1024]{1,0:T(8,128)(2,1)}, u32[]{:S(2)}) copy-start(bf16[1024,1024]{1,0:T(8,128)(2,1)} %param.29) | copy-start | bytes 6291460
Sparse Core Ops, SparseCore 0:
  12.7 30.5 all-gather.2
  96.7 50.6 reduce-scatter.7
  156.8 27.8 all-gather.4
  226.4 41.2 reduce-scatter.9
  273.5 101.9 reduce-scatter.13
  378.2 139.7 reduce-scatter.15
  520.9 136.6 reduce-scatter.17
  660.4 136.5 reduce-scatter.19
  799.9 136.7 reduce-scatter.11
where the time goes:
time: 952 us; the launch traced here: 944 us
  waiting for transfers between devices  685 us (72%)
  matrix products  107 us (11%)
  blocking collectives  79.1 us (8%)
  other arithmetic  26.1 us (3%)
  local copies, waits for them, and re-layouts  22.3 us (2%)
  between operations  14.7 us (2%)
    reduce_scatter x1, waiting for transfers between devices, body(): lax.psum_scatter(out_weight_grad, ('batch', 'seq'), scatter_dimension=0,...  143 us
    reduce_scatter x1, waiting for transfers between devices, body(): lax.psum_scatter(query_weight_grad, ('batch', 'seq'), scatter_dimension=0...  140 us
    reduce_scatter x1, waiting for transfers between devices, body(): lax.psum_scatter(up_grad, ('batch', 'seq'), scatter_dimension=0, tiled=True)  140 us
    reduce_scatter x1, waiting for transfers between devices, body(): lax.psum_scatter(down_grad, ('batch', 'seq'), scatter_dimension=0, tiled=...  139 us
    reduce_scatter x1, waiting for transfers between devices, body(): lax.psum_scatter(matmul(probs_low, value_rows), 'seq', scatter_dimension=...  50.8 us
    reduce_scatter x1, waiting for transfers between devices, body(): lax.psum_scatter(kv_weight_grad, ('batch', 'seq'), scatter_dimension=1, t...  44.5 us
    unnamed x1, blocking collectives  39.4 us
    dot_general x7, matrix products, matmul(): return jnp.dot(operand, factor, preferred_element_type=jnp.float32)  39 us
  transfers between devices with their start and end apart: 9, of which 8 were waited for; matrix products, arithmetic and copies ran while one was open for 9% of the time, Pallas kernels for 0%

commit v1 on v0

v1 whole, which is shorter than its diff:
```python
import functools
import math
from types import SimpleNamespace

import jax
import jax.numpy as jnp
import numpy as np
from jax import lax
from jax.experimental import pallas as pl
from jax.experimental.pallas import tpu as pltpu
from jax.sharding import PartitionSpec as P

IMG_W = 32
TOP_FREQ = 112.0
TINY = 1e-05
FLOOR = -1e30
MESH = pl.DeviceIdType.MESH
F32 = jnp.float32
BF16 = jnp.bfloat16
LANES = 128
CELLS = IMG_W * IMG_W
SMALL_ORDER = ("c", "b", "a", "z")
COLOR = 2 * IMG_W
ONE = COLOR + 3


def position_tables(feat):
    bands = (feat - 5) // 4
    freq = np.linspace(1.0, TOP_FREQ, bands).astype(np.float32)
    grid = (np.float32(2.0) * np.arange(IMG_W, dtype=np.float32) / np.float32(IMG_W - 1) - np.float32(1.0)).astype(np.float32)
    phase = ((np.float32(math.pi) * grid)[:, None] * freq[None, :]).astype(np.float64)
    table = np.zeros((LANES, feat), np.float64)
    for axis in range(2):
        rows = slice(axis * IMG_W, (axis + 1) * IMG_W)
        table[rows, 3 + axis] = grid
        table[rows, 5 + axis * bands : 5 + (axis + 1) * bands] = np.sin(phase)
        table[rows, 5 + (2 + axis) * bands : 5 + (3 + axis) * bands] = np.cos(phase)
    for channel in range(3):
        table[COLOR + channel, channel] = 1.0
    centered = table - table.mean(axis=1, keepdims=True)
    gram = centered @ centered.T / feat
    place = np.arange(CELLS)
    row, col = place // IMG_W, IMG_W + place % IMG_W
    geometry = np.zeros((8, CELLS), np.float32)
    geometry[0] = gram[row, row] + gram[col, col] + 2.0 * gram[row, col]
    for channel in range(3):
        geometry[1 + channel] = gram[COLOR + channel, row] + gram[COLOR + channel, col]
    wide = -(-feat // LANES) * LANES
    padded = np.zeros((LANES, wide), np.float32)
    padded[:, :feat] = centered
    turned = np.zeros((wide + 8, LANES), np.float32)
    turned[:feat] = centered.T
    turned[wide, ONE] = 1.0
    high = turned.astype(jnp.bfloat16)
    low = (turned - high.astype(np.float32)).astype(jnp.bfloat16)
    colors = gram[COLOR : COLOR + 3, COLOR : COLOR + 3]
    return padded, geometry, np.concatenate([high, low], axis=1), [[float(v) for v in line] for line in colors]


def split(values):
    high = values.astype(BF16)
    return high, (values - high.astype(F32)).astype(BF16)


def dot_nn(left, right):
    return jnp.dot(left, right, preferred_element_type=F32)


def dot_nt(left, right):
    return lax.dot_general(left, right, (((1,), (1,)), ((), ())), preferred_element_type=F32)


def dot_tn(left, right):
    return lax.dot_general(left, right, (((0,), (0,)), ((), ())), preferred_element_type=F32)


def plan(n_batch, n_seq, width):
    core = 2
    fast = math.isqrt(n_seq // core)
    while (n_seq // core) % fast:
        fast -= 1
    slow = n_seq // core // fast
    sizes = {"z": n_batch, "a": slow, "b": fast, "c": core}
    parts, left = dict(sizes), width
    for name in ("c", "b", "a"):
        if width // math.prod(parts.values()) < 16:
            parts[name] = 1
    orders = (("b", "a") if parts["b"] > 1 else ("a", "b"), ("a", "b"))
    return sizes, parts, width // math.prod(parts.values()), orders


def shapes_of(n_batch, n_seq, width, pix_dev, n_img, feat):
    sizes, parts, rows, orders = plan(n_batch, n_seq, width)
    img = -(-n_img // 16) * 16
    blocks = pix_dev // LANES
    wide = -(-feat // LANES) * LANES
    factor_rows = (width // (2 * rows), 2, rows) if parts["c"] > 1 else (1, 1, width)
    S = SimpleNamespace()
    vm = lambda *shape, dtype=BF16: pltpu.VMEM(shape, dtype)
    S.wq, S.wo, S.wu, S.wd = [vm(width, width)] * 4
    S.tk = vm(3 * LANES, width)
    S.tv = vm(3 * LANES, width)
    S.ee = vm(2 * LANES, CELLS)
    S.mt = vm(LANES, wide, dtype=F32)
    S.xl, S.xm, S.res, S.ag = [vm(LANES, width, dtype=F32)] * 4
    S.rl = vm(LANES, LANES, dtype=F32)
    S.rm = vm(LANES, LANES, dtype=F32)
    S.nl, S.q, S.merged, S.nm, S.act, S.da = [vm(LANES, width)] * 6
    S.pb = vm(3, n_seq * blocks, LANES)
    S.sel = vm(9 * img, n_seq * blocks)
    S.xi = vm(3, img, CELLS)
    S.ri = vm(img, CELLS, dtype=F32)
    S.xx = vm(3, LANES, CELLS)
    S.rr = vm(LANES, CELLS, dtype=F32)
    S.ss = vm(LANES, CELLS, dtype=F32)
    S.pp = vm(LANES, CELLS, dtype=F32)
    S.low = vm(LANES, CELLS)
    S.dp = vm(2 * LANES, CELLS)
    S.ye = vm(LANES, CELLS)
    S.side = vm(LANES, LANES, dtype=F32)
    S.owner = vm(LANES, LANES, dtype=F32)
    S.pg = vm(9 * img, LANES, dtype=F32)
    S.pgs = vm(3, n_seq * blocks, LANES, dtype=F32)
    S.pgr = vm(n_seq - 1, 3, blocks, LANES, dtype=F32)
    S.at = vm(4, *factor_rows, 2 * LANES)
    S.bt = vm(4, 2 * LANES, width)
    S.zt = vm(2 * width, LANES)
    S.ms0 = vm(4, parts["z"], parts["a"], parts["b"], rows, width)
    S.zs0 = vm(1, parts["z"], parts["a"], parts["b"], 2 * rows, LANES)
    S.mr, S.zr = [], []
    for made, mats, across in ((S.mr, 4, width // 2), (S.zr, 1, LANES)):
        for first, other in orders:
            made.append([
                vm(mats, sizes[first] - 1, parts["z"], parts[other], rows, across),
                vm(mats, sizes[other] - 1, parts["z"], rows, across),
                vm(mats, sizes["z"] - 1, rows, across),
            ])
    S.zc = vm(parts["z"], parts["a"], parts["b"], parts["c"], 2 * rows, LANES)
    S.zcr = vm(parts["z"], parts["a"], parts["b"], 2 * rows, LANES)
    S.out = vm(4, rows, width, dtype=F32)
    S.zout = vm(2 * rows, LANES, dtype=F32)
    S.ar = vm(5, 8, width, dtype=F32)
    S.arr = [vm(sizes[name] - 1, 8, width, dtype=F32) for name in SMALL_ORDER]
    most = max(sizes.values()) - 1
    sem = lambda *shape: pltpu.SemaphoreType.DMA(shape)
    S.w_sem = sem(4)
    S.px_s, S.px_r = sem(n_seq - 1), sem(n_seq - 1)
    S.pg_s, S.pg_r = sem(n_seq - 1), sem(n_seq - 1)
    S.co_s, S.co_r = sem(9), sem(9)
    S.rs_s, S.rs_r = sem(5, 2, 3, most), sem(5, 2, 3, most)
    S.ar_s, S.ar_r = sem(4, most), sem(4, most)
    return S


def layer(
    n_batch, n_seq, width, n_img, feat, gram,
    lat, px, cnt, img_of, qgain, qshift, hwq, igain, ishift, kvw, hwo, mgain, mshift, hwu, hwd, cot, fc, geo, fct,
    o_mixed, o_lat, o_pix, o_vec, o_wq, o_in, o_kv, o_wo, o_wu, o_wd, r,
):
    r = SimpleNamespace(**r)
    sizes, parts, rows, orders = plan(n_batch, n_seq, width)
    img = r.xi.shape[1]
    blocks = px.shape[1]
    wide = r.mt.shape[1]
    span = CELLS + LANES
    scale = width ** (-0.5)

    z = lax.axis_index("batch")
    s = lax.axis_index("seq")
    c = lax.rem(s, 2)
    b = lax.rem(s // 2, sizes["b"])
    a = s // (2 * sizes["b"])
    here = {"z": z, "a": a, "b": b, "c": c}

    def device(**moved):
        at = {**here, **moved}
        return (at["z"], (at["a"] * sizes["b"] + at["b"]) * 2 + at["c"])

    def part(name, index):
        return index if parts[name] > 1 else 0

    def peer(name, offset):
        return lax.rem(here[name] + offset, sizes[name])

    barrier = pltpu.get_barrier_semaphore()
    for offset in range(1, n_seq):
        pl.semaphore_signal(barrier, inc=1, device_id=(z, lax.rem(s + offset, n_seq)), device_id_type=MESH)
    for offset in range(1, n_batch):
        pl.semaphore_signal(barrier, inc=1, device_id=(peer("z", offset), s), device_id_type=MESH)

    weights = []
    for i, (src, dst) in enumerate(((hwq, r.wq), (hwd, r.wd), (hwo, r.wo), (hwu, r.wu))):
        copy = pltpu.make_async_copy(src, dst, r.w_sem.at[i])
        copy.start()
        weights.append(copy)

    tile = 16

    def by_rows(step):
        def run(i, carry):
            step(pl.ds(pl.multiple_of(i * tile, tile), tile))
            return carry

        lax.fori_loop(0, LANES // tile, run, 0)

    mine = pl.ds(pl.multiple_of(c * LANES, LANES), LANES)

    def turn(which, factor):
        for j in range(width // LANES):
            block = factor[:, j * LANES : (j + 1) * LANES].astype(F32).T.astype(BF16)
            if parts["c"] > 1:
                deep = LANES // (2 * rows)
                r.at[which, j * deep : (j + 1) * deep, :, :, mine] = block.reshape(deep, 2, rows, LANES)
            else:
                r.at[which, 0, 0, j * LANES : (j + 1) * LANES, mine] = block

    core_copies = {}

    def to_core(key, index, src, dst):
        copy = pltpu.make_async_remote_copy(
            src_ref=src, dst_ref=dst, send_sem=r.co_s.at[index], recv_sem=r.co_r.at[index],
            device_id=device(c=1 - c), device_id_type=MESH,
        )
        copy.start()
        core_copies[key] = copy

    def send_left(which):
        ref = r.at.at[which, :, part("c", 1 - c), :, mine]
        to_core(("left", which), 2 * which, ref, ref)

    def send_right(which):
        ref = r.bt.at[which, mine, :]
        to_core(("right", which), 2 * which + 1, ref, ref)

    def norm_latents(at):
        x = lat[0, at, :].astype(F32)
        center = x - jnp.mean(x, axis=-1, keepdims=True)
        inv = lax.rsqrt(jnp.mean(center * center, axis=-1, keepdims=True) + TINY)
        hat = center * inv
        r.xl[at, :] = hat
        r.rl[at, :] = jnp.broadcast_to(inv, (tile, LANES))
        r.nl[at, :] = (hat * qgain[...] + qshift[...]).astype(BF16)

    by_rows(norm_latents)
    DOWN, UP, OUT, QUERY = 0, 1, 2, 3
    turn(QUERY, r.nl)
    r.bt[DOWN, mine, :] = cot[0]

    pl.semaphore_wait(barrier, n_seq - 1 + n_batch - 1)

    own = pl.ds(pl.multiple_of(s * blocks, blocks), blocks)
    pixel_copies = []
    for offset in range(1, n_seq):
        copy = pltpu.make_async_remote_copy(
            src_ref=px, dst_ref=r.pb.at[:, own, :],
            send_sem=r.px_s.at[offset - 1], recv_sem=r.px_r.at[n_seq - offset - 1],
            device_id=(z, lax.rem(s + offset, n_seq)), device_id_type=MESH,
        )
        copy.start()
        pixel_copies.append(copy)
    r.pb[:, own, :] = px[...]
    send_left(QUERY)
    send_right(DOWN)

    row_of = lax.broadcasted_iota(jnp.int32, (LANES, feat), 0)
    code = fc[:, :feat] * igain[...] + jnp.where(row_of == ONE, ishift[...], 0.0)
    r.mt[...] = jnp.zeros_like(r.mt)
    r.mt[:, :feat] = code
    code_high, code_low = split(code)
    code_both = jnp.concatenate([code_high, code_low], axis=0)
    for table, base in ((r.tk, 0), (r.tv, width)):
        for j in range(0, width, 256):
            both = dot_nn(code_both, kvw[:, base + j : base + j + 256])
            high, low = split(both[:LANES] + both[LANES:])
            table[:LANES, j : j + 256] = high
            table[LANES : 2 * LANES, j : j + 256] = low
            table[2 * LANES :, j : j + 256] = high
    cell = lax.broadcasted_iota(jnp.int32, (LANES, CELLS), 1)
    line = lax.broadcasted_iota(jnp.int32, (LANES, CELLS), 0)
    hit = (line == cell // IMG_W) | (line == IMG_W + lax.rem(cell, IMG_W))
    grid_code = jnp.where(hit, 1.0, 0.0).astype(BF16)
    r.ee[:LANES, :] = grid_code
    r.ee[LANES:, :] = grid_code

    weights[0].wait()
    for j in range(0, width, 256):
        r.q[:, j : j + 256] = dot_nn(r.nl[...], r.wq[:, j : j + 256]).astype(BF16)
    query_code = dot_nt(r.q[...], r.tk[: 2 * LANES, :])
    query_code = (query_code[:, :LANES] + query_code[:, LANES:]) * scale

    weights[1].wait()
    for j in range(0, width, 256):
        r.ag[:, j : j + 256] = dot_nt(cot[0], r.wd[j : j + 256, :])

    counts_row = cnt[...].astype(F32)
    number = lax.broadcasted_iota(jnp.int32, (img, n_img), 0)
    against = lax.broadcasted_iota(jnp.int32, (img, n_img), 1)
    counts_all = jnp.broadcast_to(counts_row, (img, n_img))
    first = jnp.sum(jnp.where(against < number, counts_all, 0.0), axis=1, keepdims=True).astype(jnp.int32)
    count = jnp.sum(jnp.where(against == number, counts_all, 0.0), axis=1, keepdims=True).astype(jnp.int32)
    block_of = first // LANES
    shift_of = lax.rem(first, LANES)
    block_id = lax.broadcasted_iota(jnp.int32, (img, n_seq * blocks), 1)
    for j in range(9):
        r.sel[j * img : (j + 1) * img, :] = jnp.where(block_id == block_of + j, 1.0, 0.0).astype(BF16)

    mine_lat = pl.ds(pl.multiple_of(s * LANES, LANES), LANES)
    owner_row = img_of[:, mine_lat].astype(F32)
    square0 = lax.broadcasted_iota(jnp.int32, (LANES, LANES), 0)
    square1 = lax.broadcasted_iota(jnp.int32, (LANES, LANES), 1)
    diagonal = square0 == square1
    owner = jnp.sum(jnp.where(diagonal, jnp.broadcast_to(owner_row, (LANES, LANES)), 0.0), axis=1, keepdims=True)
    owner_i = owner.astype(jnp.int32)
    pick = jnp.where(lax.broadcasted_iota(jnp.int32, (LANES, img), 1) == owner_i, 1.0, 0.0).astype(BF16)
    pick_t = jnp.where(
        lax.broadcasted_iota(jnp.int32, (img, LANES), 0) == owner_row.astype(jnp.int32), 1.0, 0.0
    )
    count_lat = jnp.sum(
        jnp.where(lax.broadcasted_iota(jnp.int32, (LANES, n_img), 1) == owner_i, jnp.broadcast_to(counts_row, (LANES, n_img)), 0.0),
        axis=1, keepdims=True,
    )
    r.owner[...] = jnp.broadcast_to(count_lat, (LANES, LANES))

    for copy in pixel_copies:
        copy.wait()

    inside = lax.broadcasted_iota(jnp.int32, (img, CELLS), 1) < count
    for channel in range(3):
        rows_of = dot_nn(r.sel[...], r.pb[channel])
        window = jnp.concatenate([rows_of[j * img : (j + 1) * img] for j in range(9)], axis=1)
        for bit in range(7):
            step = 1 << bit
            moved = pltpu.roll(window, span - step, 1)
            window = jnp.where((shift_of & step) != 0, moved, window)
        r.xi[channel] = jnp.where(inside, window[:, :CELLS], 0.0).astype(BF16)

    def gram_row(channel, x):
        base = geo[1 + channel : 2 + channel, :]
        return base, base + gram[channel][0] * x[0] + gram[channel][1] * x[1] + gram[channel][2] * x[2]

    for at in range(0, img, 16):
        x = [r.xi[channel, at : at + 16, :].astype(F32) for channel in range(3)]
        square = jnp.broadcast_to(geo[0:1, :], (16, CELLS))
        for channel in range(3):
            base, u = gram_row(channel, x)
            square = square + x[channel] * (base + u)
        r.ri[at : at + 16, :] = lax.rsqrt(square + TINY)
    for channel in range(3):
        r.xx[channel] = dot_nn(pick, r.xi[channel]).astype(BF16)
    inv_high, inv_low = split(r.ri[...])
    r.rr[...] = dot_nn(pick, inv_high) + dot_nn(pick, inv_low)

    def over_grid(code):
        return jnp.concatenate(split(code), axis=1)

    r.ss[...] = dot_nn(over_grid(query_code), r.ee[...])
    r.side[...] = query_code
    lane = lax.broadcasted_iota(jnp.int32, (tile, LANES), 1)
    place = lax.broadcasted_iota(jnp.int32, (tile, CELLS), 1).astype(F32)

    def side_columns(code, one, sums):
        made = jnp.where(lane == ONE, one, 0.0)
        for channel in range(3):
            made = made + jnp.where(lane == COLOR + channel, sums[channel], 0.0)
        return made

    def attend(at):
        code = r.side[at, :]
        x = [r.xx[channel, at, :].astype(F32) for channel in range(3)]
        inv = r.rr[at, :]
        raw = r.ss[at, :]
        for channel in range(3):
            raw = raw + code[:, COLOR + channel : COLOR + channel + 1] * x[channel]
        r.ss[at, :] = raw
        allowed = place < r.owner[at, :1]
        score = jnp.where(allowed, raw * inv + code[:, ONE : ONE + 1], FLOOR)
        top = jnp.max(score, axis=1, keepdims=True)
        raised = jnp.where(allowed, jnp.exp(score - top), 0.0)
        total = jnp.sum(raised, axis=1, keepdims=True)
        prob = raised / total
        r.pp[at, :] = prob
        weighted = prob * inv
        r.low[at, :] = weighted.astype(BF16)
        sums = [jnp.sum(weighted * x[channel], axis=1, keepdims=True) for channel in range(3)]
        r.side[at, :] = side_columns(code, jnp.sum(prob, axis=1, keepdims=True), sums)

    by_rows(attend)
    value_code = dot_nt(r.low[...], r.ee[:LANES, :]) + r.side[...]
    code_high, code_low = split(value_code)
    code_three = jnp.concatenate([code_high, code_high, code_low], axis=1)
    for j in range(0, width, 256):
        r.merged[:, j : j + 256] = dot_nn(code_three, r.tv[:, j : j + 256]).astype(BF16)
    value_code_low = code_high

    weights[2].wait()
    for j in range(0, width, 256):
        r.res[:, j : j + 256] = lat[0, :, j : j + 256].astype(F32) + dot_nn(r.merged[...], r.wo[:, j : j + 256])

    def norm_mid(at):
        x = r.res[at, :]
        center = x - jnp.mean(x, axis=-1, keepdims=True)
        inv = lax.rsqrt(jnp.mean(center * center, axis=-1, keepdims=True) + TINY)
        hat = center * inv
        r.xm[at, :] = hat
        r.rm[at, :] = jnp.broadcast_to(inv, (tile, LANES))
        r.nm[at, :] = (hat * mgain[...] + mshift[...]).astype(BF16)

    by_rows(norm_mid)
    weights[3].wait()
    for j in range(0, width, 256):
        pre = dot_nn(r.nm[...], r.wu[:, j : j + 256])
        phi = 0.5 * (1.0 + lax.erf(pre * math.sqrt(0.5)))
        r.act[:, j : j + 256] = (pre * phi).astype(BF16)
        slope = phi + pre * (jnp.exp(-0.5 * pre * pre) * (1.0 / math.sqrt(2.0 * math.pi)))
        r.bt[UP, mine, j : j + 256] = (r.ag[:, j : j + 256] * slope).astype(BF16)
    turn(DOWN, r.act)
    send_left(DOWN)
    turn(UP, r.nm)
    send_left(UP)
    send_right(UP)
    turn(OUT, r.merged)
    send_left(OUT)

    for j in range(0, width, 256):
        o_mixed[0, :, j : j + 256] = (r.res[:, j : j + 256] + dot_nn(r.act[...], r.wd[:, j : j + 256])).astype(BF16)
    for j in range(0, width, 256):
        r.ag[:, j : j + 256] = dot_nt(r.bt[UP, mine, :], r.wu[j : j + 256, :])
    r.ar[0] = jnp.zeros_like(r.ar[0])
    zero = jnp.zeros((1, width), F32)

    def norm_back(grad, hat, inv, gain):
        scaled = grad * gain
        return inv * (scaled - jnp.mean(scaled, axis=-1, keepdims=True) - hat * jnp.mean(scaled * hat, axis=-1, keepdims=True))

    def mid_back(i, carry):
        at = pl.ds(pl.multiple_of(i * tile, tile), tile)
        grad, hat = r.ag[at, :], r.xm[at, :]
        total = cot[0, at, :].astype(F32) + norm_back(grad, hat, r.rm[at, :1], mgain[...])
        r.res[at, :] = total
        r.bt[OUT, pl.ds(pl.multiple_of(c * LANES + i * tile, tile), tile), :] = total.astype(BF16)
        return carry[0] + jnp.sum(grad * hat, axis=0, keepdims=True), carry[1] + jnp.sum(grad, axis=0, keepdims=True)

    gain_sum, shift_sum = lax.fori_loop(0, LANES // tile, mid_back, (zero, zero))
    r.ar[0, 2:3, :] = gain_sum
    r.ar[0, 3:4, :] = shift_sum
    send_right(OUT)
    for j in range(0, width, 256):
        r.da[:, j : j + 256] = dot_nt(r.bt[OUT, mine, :], r.wo[j : j + 256, :]).astype(BF16)

    back_code = dot_nt(r.da[...], r.tv[: 2 * LANES, :])
    back_code = back_code[:, :LANES] + back_code[:, LANES:]
    r.ag[...] = dot_nn(over_grid(back_code), r.ee[...])
    r.side[...] = back_code

    def attend_back(at):
        code = r.side[at, :]
        x = [r.xx[channel, at, :].astype(F32) for channel in range(3)]
        inv = r.rr[at, :]
        prob = r.pp[at, :]
        raw = r.ag[at, :]
        for channel in range(3):
            raw = raw + code[:, COLOR + channel : COLOR + channel + 1] * x[channel]
        grad = raw * inv + code[:, ONE : ONE + 1]
        delta = jnp.sum(prob * grad, axis=1, keepdims=True)
        back = prob * (grad - delta)
        r.ye[at, :] = (back * r.ss[at, :] + prob * raw).astype(BF16)
        weighted = back * inv
        r.low[at, :] = weighted.astype(BF16)
        r.dp[at, :] = back.astype(BF16)
        sums = [jnp.sum(weighted * x[channel], axis=1, keepdims=True) for channel in range(3)]
        r.side[at, :] = side_columns(code, jnp.sum(back, axis=1, keepdims=True), sums)

    by_rows(attend_back)
    r.dp[LANES:, :] = r.pp[...].astype(BF16)
    key_code = (dot_nt(r.low[...], r.ee[:LANES, :]) + r.side[...]) * scale
    code_high, code_low = split(key_code)
    code_three = jnp.concatenate([code_high, code_high, code_low], axis=1)
    for j in range(0, width, 256):
        r.bt[QUERY, mine, j : j + 256] = dot_nn(code_three, r.tk[:, j : j + 256]).astype(BF16)
    send_right(QUERY)

    for j in range(0, width, 256):
        r.zt[j : j + 256, :] = dot_tn(r.q[:, j : j + 256], code_high).astype(BF16)
        r.zt[width + j : width + j + 256, :] = dot_tn(r.da[:, j : j + 256], value_code_low).astype(BF16)
    r.zc[...] = r.zt[...].reshape(r.zc.shape)
    if parts["c"] > 1:
        to_core("z", 8, r.zc.at[:, :, :, 1 - c], r.zcr)
    else:
        to_core("z", 8, r.zc.at[:, :, :, 0], r.zcr)

    query_t, back_t = query_code.T, back_code.T
    lifted = jnp.concatenate(
        [
            jnp.concatenate([pick_t * code_t[COLOR + channel : COLOR + channel + 1, :] for code_t in (query_t, back_t)], axis=1)
            for channel in range(3)
        ],
        axis=0,
    ).astype(BF16)
    along = dot_nn(pick_t.astype(BF16), r.ye[...])
    inv = r.ri[...]
    cube = inv * inv * inv * along
    colors = [r.xi[channel].astype(F32) for channel in range(3)]
    for channel in range(3):
        steep = dot_nn(lifted[channel * img : (channel + 1) * img], r.dp[...])
        own_grad = inv * steep - cube * gram_row(channel, colors)[1]
        window = jnp.concatenate([own_grad, jnp.zeros((img, LANES), F32)], axis=1)
        for bit in range(7):
            step = 1 << bit
            moved = pltpu.roll(window, step, 1)
            window = jnp.where((shift_of & step) != 0, moved, window)
        for j in range(9):
            r.pg[j * img : (j + 1) * img, :] = window[:, j * LANES : (j + 1) * LANES]
        grad_high, grad_low = split(r.pg[...])
        r.pgs[channel] = dot_tn(r.sel[...], grad_high) + dot_tn(r.sel[...], grad_low)
    grad_copies = []
    for offset in range(1, n_seq):
        target = lax.rem(s + offset, n_seq)
        copy = pltpu.make_async_remote_copy(
            src_ref=r.pgs.at[:, pl.ds(pl.multiple_of(target * blocks, blocks), blocks), :],
            dst_ref=r.pgr.at[n_seq - offset - 1],
            send_sem=r.pg_s.at[offset - 1], recv_sem=r.pg_r.at[n_seq - offset - 1],
            device_id=(z, target), device_id_type=MESH,
        )
        copy.start()
        grad_copies.append(copy)

    in_gain, in_shift = jnp.zeros((feat, 1), F32), jnp.zeros((feat, 1), F32)
    for j in range(0, 2 * width, 256):
        sums = r.zt[j : j + 256, :]
        spread = dot_nt(fct[...], jnp.concatenate([sums, sums], axis=1))
        factor = kvw[:, j : j + 256].astype(F32)
        in_gain = in_gain + jnp.sum(factor * spread[:feat], axis=1, keepdims=True)
        in_shift = in_shift + jnp.sum(factor * spread[wide : wide + 1], axis=1, keepdims=True)
    for at, column in ((4, in_gain), (5, in_shift)):
        for j in range(0, feat, LANES):
            tall = min(LANES, feat - j)
            eye = lax.broadcasted_iota(jnp.int32, (tall, LANES), 0) == lax.broadcasted_iota(jnp.int32, (tall, LANES), 1)
            r.ar[0, at : at + 1, j : j + LANES] = jnp.sum(jnp.where(eye, column[j : j + tall], 0.0), axis=0, keepdims=True)

    for j in range(0, width, 256):
        r.ag[:, j : j + 256] = dot_nt(r.bt[QUERY, mine, :], r.wq[j : j + 256, :])

    def latents_back(i, carry):
        at = pl.ds(pl.multiple_of(i * tile, tile), tile)
        grad, hat = r.ag[at, :], r.xl[at, :]
        o_lat[0, at, :] = r.res[at, :] + norm_back(grad, hat, r.rl[at, :1], qgain[...])
        return carry[0] + jnp.sum(grad * hat, axis=0, keepdims=True), carry[1] + jnp.sum(grad, axis=0, keepdims=True)

    gain_sum, shift_sum = lax.fori_loop(0, LANES // tile, latents_back, (zero, zero))
    r.ar[0, 0:1, :] = gain_sum
    r.ar[0, 1:2, :] = shift_sum

    def start_stage(key, stage, name, src_of, dst):
        mat, half = key
        copies = []
        for offset in range(1, sizes[name]):
            target = peer(name, offset)
            slot = sizes[name] - offset - 1
            copy = pltpu.make_async_remote_copy(
                src_ref=src_of(part(name, target)), dst_ref=dst.at[slot],
                send_sem=r.rs_s.at[mat, half, stage, offset - 1], recv_sem=r.rs_r.at[mat, half, stage, slot],
                device_id=device(**{name: target}), device_id_type=MESH,
            )
            copy.start()
            copies.append(copy)
        return copies

    def wait_all(copies):
        for copy in copies:
            copy.wait()

    def gathered(own, dst, n):
        total = own.astype(F32)
        for slot in range(n - 1):
            total = total + dst[slot].astype(F32)
        return total

    flying = {}

    def buffers_of(mat):
        return (r.zs0, r.zr, 0) if mat == 4 else (r.ms0, r.mr, mat)

    def cut(mat, half):
        if mat == 4:
            return pl.ds(half * rows, rows), slice(None)
        return slice(None), pl.ds(half * (width // 2), width // 2)

    def blocks_at(mat, half, stage, target=None):
        s0, received, i = buffers_of(mat)
        at = {"z": slice(None), "a": slice(None), "b": slice(None)}
        path = orders[half] + ("z",)
        for done in path[:stage]:
            at[done] = part(done, here[done])
        at[path[stage]] = part(path[stage], here[path[stage]]) if target is None else target
        return (i, at["z"], at["a"], at["b"]) + cut(mat, half)

    def start(mat, stage):
        s0, received, i = buffers_of(mat)
        for half in range(2):
            name = (orders[half] + ("z",))[stage]
            flying[mat, half] = start_stage(
                (mat, half), stage, name,
                lambda p: s0.at[blocks_at(mat, half, stage, p)],
                received[half][stage].at[i],
            )

    def step(mat, stage):
        s0, received, i = buffers_of(mat)
        for half in range(2):
            wait_all(flying[mat, half])
            name = (orders[half] + ("z",))[stage]
            keep = blocks_at(mat, half, stage)
            total = gathered(s0[keep], received[half][stage].at[i], sizes[name])
            if stage < 2:
                s0[keep] = total.astype(BF16)
            elif mat == 4:
                r.zout[cut(mat, half)] = total
            else:
                r.out[(mat,) + cut(mat, half)] = total
        if stage < 2:
            start(mat, stage + 1)

    def product(mat):
        core_copies.pop(("left", mat)).wait()
        core_copies.pop(("right", mat)).wait()
        left = r.at[mat, :, part("c", c)].reshape(-1, 2 * LANES)
        for j in range(0, width, 256):
            made = dot_nn(left, r.bt[mat, :, j : j + 256]).astype(BF16)
            r.ms0[mat, :, :, :, :, j : j + 256] = made.reshape(parts["z"], parts["a"], parts["b"], rows, 256)

    for mat in range(4):
        product(mat)
        start(mat, 0)
    core_copies.pop("z").wait()
    r.zs0[0] = (r.zc[:, :, :, part("c", c)].astype(F32) + r.zcr[...].astype(F32)).astype(BF16)
    start(4, 0)

    small = {}

    def small_start(stage):
        name = SMALL_ORDER[stage]
        copies = []
        for offset in range(1, sizes[name]):
            slot = sizes[name] - offset - 1
            copy = pltpu.make_async_remote_copy(
                src_ref=r.ar.at[stage], dst_ref=r.arr[stage].at[slot],
                send_sem=r.ar_s.at[stage, offset - 1], recv_sem=r.ar_r.at[stage, slot],
                device_id=device(**{name: peer(name, offset)}), device_id_type=MESH,
            )
            copy.start()
            copies.append(copy)
        small[stage] = copies

    def small_end(stage):
        name = SMALL_ORDER[stage]
        wait_all(small[stage])
        total = r.ar[stage]
        for slot in range(sizes[name] - 1):
            total = total + r.arr[stage][slot]
        r.ar[stage + 1] = total

    small_start(0)
    small_end(0)
    small_start(1)
    step(0, 0)
    small_end(1)
    small_start(2)
    step(1, 0)
    small_end(2)
    small_start(3)
    step(0, 1)
    step(2, 0)
    step(1, 1)
    step(3, 0)
    step(2, 1)
    step(4, 0)
    small_end(3)
    for copy in grad_copies:
        copy.wait()
    pixel = r.pgs[:, own, :]
    for slot in range(n_seq - 1):
        pixel = pixel + r.pgr[slot]
    for channel in range(3):
        for j in range(blocks):
            o_pix[0, channel : channel + 1, j * LANES : (j + 1) * LANES] = pixel[channel, j : j + 1, :]
    step(0, 2)
    step(1, 2)
    step(3, 1)
    step(4, 1)
    step(2, 2)
    step(3, 2)
    step(4, 2)

    total_rows = width // (n_batch * n_seq)
    inner = 0
    for name in ("a", "b", "c"):
        if parts[name] < sizes[name]:
            inner = inner * sizes[name] + here[name]
    for mat, made in enumerate((o_wd, o_wu, o_wo, o_wq)):
        if total_rows == rows:
            made[...] = r.out[mat]
        else:
            made[...] = pltpu.roll(r.out[mat], lax.rem(rows - inner * total_rows, rows), 0)[:total_rows]
    index = z * n_seq + s
    turned = pltpu.roll(r.ar[4], lax.rem(width - index * total_rows, width), 1)
    o_vec[...] = turned[:4, :total_rows]
    o_in[...] = r.ar[4, 4:6, :feat]
    code_high, code_low = split(r.mt[...].T)
    spread_left = jnp.concatenate([code_high, code_high, code_low], axis=1)
    if total_rows == rows:
        sums = r.zout[...]
    else:
        sums = pltpu.roll(r.zout[...], lax.rem(2 * (rows - inner * total_rows), 2 * rows), 0)[: 2 * total_rows]
    high, low = split(sums)
    o_kv[...] = dot_nt(spread_left, jnp.concatenate([high, low, high], axis=1))[:feat]


def solution(mesh):
    n_batch, n_seq = mesh.shape["batch"], mesh.shape["seq"]

    def body(latents, pixels, counts, latent_image, query_gain, query_shift, query_weight, input_gain, input_shift,
             kv_weight, out_weight, mlp_gain, mlp_shift, up_weight, down_weight, cotangent):
        width = query_weight.shape[0]
        feat = kv_weight.shape[0]
        pix_dev = pixels.shape[2]
        n_img = counts.shape[1]
        fc, geo, fct, gram = position_tables(feat)
        scratch = shapes_of(n_batch, n_seq, width, pix_dev, n_img, feat)
        rows = width // (n_batch * n_seq)
        vm = pl.BlockSpec(memory_space=pltpu.VMEM)
        hbm = pl.BlockSpec(memory_space=pl.ANY)
        out_shape = (
            jax.ShapeDtypeStruct(latents.shape, BF16),
            jax.ShapeDtypeStruct(latents.shape, F32),
            jax.ShapeDtypeStruct(pixels.shape, F32),
            jax.ShapeDtypeStruct((4, rows), F32),
            jax.ShapeDtypeStruct((rows, width), F32),
            jax.ShapeDtypeStruct((2, feat), F32),
            jax.ShapeDtypeStruct((feat, 2 * rows), F32),
            jax.ShapeDtypeStruct((rows, width), F32),
            jax.ShapeDtypeStruct((rows, width), F32),
            jax.ShapeDtypeStruct((rows, width), F32),
        )
        args = (
            latents, pixels.reshape(3, pix_dev // LANES, LANES), counts, latent_image,
            query_gain[None], query_shift[None], query_weight, input_gain[None], input_shift[None], kv_weight,
            out_weight, mlp_gain[None], mlp_shift[None], up_weight, down_weight, cotangent,
            jnp.asarray(fc), jnp.asarray(geo), jnp.asarray(fct),
        )
        made = pl.pallas_call(
            functools.partial(layer, n_batch, n_seq, width, n_img, feat, gram),
            out_shape=out_shape,
            in_specs=[hbm if getattr(arg, "shape", ()) == (width, width) else vm for arg in args],
            out_specs=[vm] * len(out_shape),
            scratch_shapes=[vars(scratch)],
            compiler_params=pltpu.CompilerParams(
                collective_id=0, has_side_effects=True, vmem_limit_bytes=60 * 1024 * 1024
            ),
            name="layer",
        )(*args)
        mixed, latent_grad, pixel_grad, vectors, wq, inner, kv, wo, wu, wd = made
        return (
            mixed, latent_grad, pixel_grad, vectors[0], vectors[1], wq, inner[0], inner[1], kv, wo,
            vectors[2], vectors[3], wu, wd,
        )

    whole, vec = P(("batch", "seq"), None), P(("batch", "seq"))
    rowed = P("batch", "seq", None)
    return jax.shard_map(
        body,
        mesh=mesh,
        in_specs=(rowed, P("batch", None, "seq"), P("batch", None), P("batch", None)) + (P(),) * 11 + (rowed,),
        out_specs=(
            rowed, rowed, P("batch", None, "seq"), vec, vec, whole, P(), P(), P(None, ("batch", "seq")), whole,
            vec, vec, whole, whole,
        ),
        check_vma=False,
    )
```

time: 952 us -> 109 us (0.11)
  waiting for transfers between devices: 685 us -> 0 us
  matrix products: 107 us -> 0 us
  Pallas kernels: 0 us -> 91.5 us
  blocking collectives: 79.1 us -> 0 us
  other arithmetic: 26.1 us -> 0 us
  between operations: 14.7 us -> 0.68 us
    reduce_scatter x7 -> x0, waiting for transfers between devices: 656 us -> none  [the longest x1 143 us: body(): lax.psum_scatter(out_weight_grad, ('batch', 'seq'), scatter_dimension=0,...]
    dot_general x21 -> x0, matrix products: 107 us -> none  [the longest x7 39 us: matmul(): return jnp.dot(operand, factor, preferred_element_type=jnp.float32)]
    pallas_call x0 -> x1, Pallas kernels: none -> 91.5 us  [body(): pl.pallas_call(functools.partial(layer, n_batch, n_seq, width, n_img, fea...]
    unnamed x1 -> x0, blocking collectives: 39.4 us -> none
    all_gather x2 -> x0, waiting for transfers between devices: 28.2 us -> none  [the longest x1 28 us: body(): all_att_grads = lax.all_gather(att_grad, 'seq', axis=0, tiled=True)]
    psum x2 -> x0, blocking collectives: 24.9 us -> none  [the longest x1 13.1 us: body(): delta_all = lax.psum(delta_part, 'seq')]
    reduce_sum x12 -> x0, other arithmetic: 15.5 us -> none  [the longest x5 6.97 us: norm_rows(): center = values - jnp.mean(values, axis=-1, keepdims=True)]
    pmax x1 -> x0, blocking collectives: 14.8 us -> none  [body(): row_top = lax.pmax(local_top, 'seq')]
  transfers between devices with their start and end apart: 9 -> 0, of which waited for: 8 -> 0; matrix products, arithmetic and copies ran while one was open for 9% -> 0% of each run, Pallas kernels for 0% -> 0%
where the time goes in v1:
time: 109 us
  Pallas kernels  91.5 us (84%)
  local copies, waits for them, and re-layouts  16.6 us (15%)
    pallas_call x1, Pallas kernels, body(): pl.pallas_call(functools.partial(layer, n_batch, n_seq, width, n_img, fea...  91.5 us
    unnamed x15, local copies, waits for them, and re-layouts  11.5 us

profile of v1, /device:TPU:0, one launch (start us, length us, event | category | flops | bytes accessed | tf_op | source)
XLA Modules:
  0.0 108.8 jit_solution(5519361451211078285)
XLA Ops:
  0.6 1.2 %broadcast_in_dim.20.igain = f32[1,261]{1,0:T(1,128)} reshape(f32[261]{0:T(512)} %param.26) | data formatting | bytes 2088 | tf_op jit(solution)/shard_map/broadcast_in_dim | solution.py:746
  1.9 1.2 %broadcast_in_dim.21.ishift = f32[1,261]{1,0:T(1,128)} reshape(f32[261]{0:T(512)} %param.27) | data formatting | bytes 2088 | tf_op jit(solution)/shard_map/broadcast_in_dim | solution.py:746
  3.1 1.3 %copy.37 = bf16[1,3,16,128]{3,2,1,0:T(8,128)(2,1)} copy(bf16[1,3,16,128]{3,1,2,0:T(4,128)(2,1)} %bitcast.18) | data formatting | bytes 24576
  4.5 91.5 %layer.1 = (bf16[1,128,1024]{2,1,0:T(8,128)(2,1)}, f32[1,128,1024]{2,1,0:T(8,128)}, f32[1,3,2048]{2,1,0:T(4,128)}, f32[4,32]{1,0:T(4,128)}, f32[32,1024]{1,0:T(8...) custom-call(bf16[1,128,1024]{2,1,0:T(8,128)(2,1)} %lat.1, ...), custom_call_target="tpu_custom_call" | custom-call | tf_op jit(solution)/shard_map/layer/pallas_call | solution.py:750
  96.0 0.0 copy-start.2
  96.0 0.0 copy-start.1
  96.0 0.0 copy-start
  96.0 1.3 %slice_bitcast_fusion = (f32[32]{0:T(128)}, f32[32]{0:T(128)}, f32[32]{0:T(128)}, f32[32]{0:T(128)}) fusion(f32[4,32]{1,0:T(4,128)} %get-tuple-element.27), kind=kLoop, calls=%fused_computation.3 | loop fusion | bytes 1024 | tf_op jit(solution)/shard_map/squeeze | solution.py:764
  97.3 1.3 %slice_reduce_fusion = (f32[261]{0:T(512)}, f32[261]{0:T(512)}) fusion(f32[2,261]{1,0:T(2,128)} %get-tuple-element.29), kind=kLoop, calls=%fused_computation.1 | loop fusion | bytes 4176 | tf_op jit(solution)/shard_map/slice | solution.py:763
  98.7 1.4 %copy.33 = f32[1,3,2048]{2,0,1:T(1,128)} copy(f32[1,3,2048]{2,1,0:T(4,128)} %get-tuple-element.36) | data formatting | bytes 49152
  100.1 1.7 %copy.34 = f32[261,64]{0,1:T(8,128)} copy(f32[261,64]{1,0:T(8,128)} %get-tuple-element.42) | data formatting | bytes 133632
  101.7 1.7 %copy.44 = bf16[1,128,1024]{2,1,0:T(8,128)(2,1)} copy(bf16[1,128,1024]{2,1,0:T(8,128)(2,1)} %get-tuple-element.68) | data formatting | bytes 524288
  103.4 1.9 %copy.45 = f32[1,128,1024]{2,1,0:T(8,128)} copy(f32[1,128,1024]{2,1,0:T(8,128)} %get-tuple-element.69) | data formatting | bytes 1048576
  105.3 1.6 %copy.46 = f32[32,1024]{1,0:T(8,128)} copy(f32[32,1024]{1,0:T(8,128)} %get-tuple-element.73) | data formatting | bytes 262144
  106.9 0.0 copy-done.2
  106.9 0.7 copy.47
  107.5 0.0 copy-done.1
  107.5 0.7 copy.48
  108.2 0.0 copy-done
  108.2 0.7 copy.49
Async XLA Ops:
  96.0 10.9 %copy-start.2 = (f32[32,1024]{1,0:T(8,128)S(1)}, f32[32,1024]{1,0:T(8,128)}, u32[]{:S(2)}) copy-start(f32[32,1024]{1,0:T(8,128)} %get-tuple-element.77) | copy-start | bytes 393220
  96.0 11.5 %copy-start.1 = (f32[32,1024]{1,0:T(8,128)S(1)}, f32[32,1024]{1,0:T(8,128)}, u32[]{:S(2)}) copy-start(f32[32,1024]{1,0:T(8,128)} %get-tuple-element.80) | copy-start | bytes 393220
  96.0 12.2 %copy-start = (f32[32,1024]{1,0:T(8,128)S(1)}, f32[32,1024]{1,0:T(8,128)}, u32[]{:S(2)}) copy-start(f32[32,1024]{1,0:T(8,128)} %get-tuple-element.81) | copy-start | bytes 393220

commit v2 on v1

--- a/solution.py
+++ b/solution.py
@@ -19,7 +19,6 @@
 BF16 = jnp.bfloat16
 LANES = 128
 CELLS = IMG_W * IMG_W
-SMALL_ORDER = ("c", "b", "a", "z")
 COLOR = 2 * IMG_W
 ONE = COLOR + 3
 
@@ -124,7 +123,6 @@
     S.pgr = vm(n_seq - 1, 3, blocks, LANES, dtype=F32)
     S.at = vm(4, *factor_rows, 2 * LANES)
     S.bt = vm(4, 2 * LANES, width)
-    S.zt = vm(2 * width, LANES)
     S.ms0 = vm(4, parts["z"], parts["a"], parts["b"], rows, width)
     S.zs0 = vm(1, parts["z"], parts["a"], parts["b"], 2 * rows, LANES)
     S.mr, S.zr = [], []
@@ -135,32 +133,40 @@
                 vm(mats, sizes[other] - 1, parts["z"], rows, across),
                 vm(mats, sizes["z"] - 1, rows, across),
             ])
-    S.zc = vm(parts["z"], parts["a"], parts["b"], parts["c"], 2 * rows, LANES)
-    S.zcr = vm(parts["z"], parts["a"], parts["b"], 2 * rows, LANES)
+    S.zc = vm(width // (rows * parts["c"]), parts["c"], 2 * rows, LANES)
+    S.zcr = vm(width // (rows * parts["c"]), 2 * rows, LANES)
+    S.vec = vm(LANES, width, dtype=F32)
     S.out = vm(4, rows, width, dtype=F32)
     S.zout = vm(2 * rows, LANES, dtype=F32)
-    S.ar = vm(5, 8, width, dtype=F32)
-    S.arr = [vm(sizes[name] - 1, 8, width, dtype=F32) for name in SMALL_ORDER]
+    S.ar = vm(2, 2, wide, dtype=F32)
+    S.ars = vm(n_seq - 1, 2, wide, dtype=F32)
+    S.arz = vm(n_batch - 1, 2, wide, dtype=F32)
+    S.lat, S.cot = [vm(LANES, width)] * 2
+    S.kvw = vm(feat, 2 * width)
+    S.fc = vm(LANES, wide, dtype=F32)
+    S.fct = vm(wide + 8, 2 * LANES)
     most = max(sizes.values()) - 1
     sem = lambda *shape: pltpu.SemaphoreType.DMA(shape)
-    S.w_sem = sem(4)
+    S.w_sem = sem(9)
+    S.o_sem = sem(6)
     S.px_s, S.px_r = sem(n_seq - 1), sem(n_seq - 1)
     S.pg_s, S.pg_r = sem(n_seq - 1), sem(n_seq - 1)
     S.co_s, S.co_r = sem(9), sem(9)
     S.rs_s, S.rs_r = sem(5, 2, 3, most), sem(5, 2, 3, most)
-    S.ar_s, S.ar_r = sem(4, most), sem(4, most)
+    S.as_s, S.as_r = sem(n_seq - 1), sem(n_seq - 1)
+    S.az_s, S.az_r = sem(n_batch - 1), sem(n_batch - 1)
     return S
 
 
 def layer(
     n_batch, n_seq, width, n_img, feat, gram,
-    lat, px, cnt, img_of, qgain, qshift, hwq, igain, ishift, kvw, hwo, mgain, mshift, hwu, hwd, cot, fc, geo, fct,
+    h_lat, px, cnt, img_of, qgain, qshift, h_wq, igain, ishift, h_kvw, h_wo, mgain, mshift, h_wu, h_wd, h_cot, h_fc, geo, h_fct,
     o_mixed, o_lat, o_pix, o_vec, o_wq, o_in, o_kv, o_wo, o_wu, o_wd, r,
 ):
     r = SimpleNamespace(**r)
     sizes, parts, rows, orders = plan(n_batch, n_seq, width)
     img = r.xi.shape[1]
-    blocks = px.shape[1]
+    blocks = px.shape[2] // LANES
     wide = r.mt.shape[1]
     span = CELLS + LANES
     scale = width ** (-0.5)
@@ -188,11 +194,21 @@
     for offset in range(1, n_batch):
         pl.semaphore_signal(barrier, inc=1, device_id=(peer("z", offset), s), device_id_type=MESH)
 
-    weights = []
-    for i, (src, dst) in enumerate(((hwq, r.wq), (hwd, r.wd), (hwo, r.wo), (hwu, r.wu))):
+    arriving = []
+    for i, (src, dst) in enumerate((
+        (h_lat.at[0], r.lat), (h_fc, r.fc), (h_kvw, r.kvw), (h_wq, r.wq), (h_cot.at[0], r.cot), (h_wd, r.wd),
+        (h_wo, r.wo), (h_wu, r.wu), (h_fct, r.fct),
+    )):
         copy = pltpu.make_async_copy(src, dst, r.w_sem.at[i])
         copy.start()
-        weights.append(copy)
+        arriving.append(copy)
+    LAT, FC, KVW, WQ, COT, WD, WO, WU, FCT = arriving
+    leaving = []
+
+    def leave(src, dst):
+        copy = pltpu.make_async_copy(src, dst, r.o_sem.at[len(leaving)])
+        copy.start()
+        leaving.append(copy)
 
     tile = 16
 
@@ -232,8 +248,86 @@
         ref = r.bt.at[which, mine, :]
         to_core(("right", which), 2 * which + 1, ref, ref)
 
+    def start_stage(key, stage, name, src_of, dst):
+        mat, half = key
+        copies = []
+        for offset in range(1, sizes[name]):
+            target = peer(name, offset)
+            slot = sizes[name] - offset - 1
+            copy = pltpu.make_async_remote_copy(
+                src_ref=src_of(part(name, target)), dst_ref=dst.at[slot],
+                send_sem=r.rs_s.at[mat, half, stage, offset - 1], recv_sem=r.rs_r.at[mat, half, stage, slot],
+                device_id=device(**{name: target}), device_id_type=MESH,
+            )
+            copy.start()
+            copies.append(copy)
+        return copies
+
+    def wait_all(copies):
+        for copy in copies:
+            copy.wait()
+
+    def gathered(own, dst, n):
+        total = own.astype(F32)
+        for slot in range(n - 1):
+            total = total + dst[slot].astype(F32)
+        return total
+
+    flying = {}
+
+    def buffers_of(mat):
+        return (r.zs0, r.zr, 0) if mat == 4 else (r.ms0, r.mr, mat)
+
+    def cut(mat, half):
+        if mat == 4:
+            return pl.ds(half * rows, rows), slice(None)
+        return slice(None), pl.ds(half * (width // 2), width // 2)
+
+    def blocks_at(mat, half, stage, target=None):
+        s0, received, i = buffers_of(mat)
+        at = {"z": slice(None), "a": slice(None), "b": slice(None)}
+        path = orders[half] + ("z",)
+        for done in path[:stage]:
+            at[done] = part(done, here[done])
+        at[path[stage]] = part(path[stage], here[path[stage]]) if target is None else target
+        return (i, at["z"], at["a"], at["b"]) + cut(mat, half)
+
+    def start(mat, stage):
+        s0, received, i = buffers_of(mat)
+        for half in range(2):
+            name = (orders[half] + ("z",))[stage]
+            flying[mat, half] = start_stage(
+                (mat, half), stage, name,
+                lambda p: s0.at[blocks_at(mat, half, stage, p)],
+                received[half][stage].at[i],
+            )
+
+    def step(mat, stage):
+        s0, received, i = buffers_of(mat)
+        for half in range(2):
+            wait_all(flying[mat, half])
+            name = (orders[half] + ("z",))[stage]
+            keep = blocks_at(mat, half, stage)
+            total = gathered(s0[keep], received[half][stage].at[i], sizes[name])
+            if stage < 2:
+                s0[keep] = total.astype(BF16)
+            elif mat == 4:
+                r.zout[cut(mat, half)] = total
+            else:
+                r.out[(mat,) + cut(mat, half)] = total
+        if stage < 2:
+            start(mat, stage + 1)
+
+    def product(mat):
+        core_copies.pop(("left", mat)).wait()
+        core_copies.pop(("right", mat)).wait()
+        left = r.at[mat, :, part("c", c)].reshape(-1, 2 * LANES)
+        for j in range(0, width, 256):
+            made = dot_nn(left, r.bt[mat, :, j : j + 256]).astype(BF16)
+            r.ms0[mat, :, :, :, :, j : j + 256] = made.reshape(parts["z"], parts["a"], parts["b"], rows, 256)
+
     def norm_latents(at):
-        x = lat[0, at, :].astype(F32)
+        x = r.lat[at, :].astype(F32)
         center = x - jnp.mean(x, axis=-1, keepdims=True)
         inv = lax.rsqrt(jnp.mean(center * center, axis=-1, keepdims=True) + TINY)
         hat = center * inv
@@ -241,36 +335,44 @@
         r.rl[at, :] = jnp.broadcast_to(inv, (tile, LANES))
         r.nl[at, :] = (hat * qgain[...] + qshift[...]).astype(BF16)
 
+    LAT.wait()
+    DOWN, UP, OUT, QUERY, SUMS = range(5)
     by_rows(norm_latents)
-    DOWN, UP, OUT, QUERY = 0, 1, 2, 3
     turn(QUERY, r.nl)
-    r.bt[DOWN, mine, :] = cot[0]
-
+    COT.wait()
+    r.bt[DOWN, mine, :] = r.cot[...]
+
+    own = pl.ds(pl.multiple_of(s * blocks, blocks), blocks)
+    colors = px[0].astype(F32)
+    for channel in range(3):
+        line = colors[channel : channel + 1]
+        stacked = jnp.concatenate([line[:, j * LANES : (j + 1) * LANES] for j in range(blocks)], axis=0)
+        r.pb[channel, own, :] = stacked.astype(BF16)
     pl.semaphore_wait(barrier, n_seq - 1 + n_batch - 1)
-
-    own = pl.ds(pl.multiple_of(s * blocks, blocks), blocks)
     pixel_copies = []
     for offset in range(1, n_seq):
         copy = pltpu.make_async_remote_copy(
-            src_ref=px, dst_ref=r.pb.at[:, own, :],
+            src_ref=r.pb.at[:, own, :], dst_ref=r.pb.at[:, own, :],
             send_sem=r.px_s.at[offset - 1], recv_sem=r.px_r.at[n_seq - offset - 1],
             device_id=(z, lax.rem(s + offset, n_seq)), device_id_type=MESH,
         )
         copy.start()
         pixel_copies.append(copy)
-    r.pb[:, own, :] = px[...]
     send_left(QUERY)
     send_right(DOWN)
 
+    FCT.wait()
+    FC.wait()
+    KVW.wait()
     row_of = lax.broadcasted_iota(jnp.int32, (LANES, feat), 0)
-    code = fc[:, :feat] * igain[...] + jnp.where(row_of == ONE, ishift[...], 0.0)
+    code = r.fc[:, :feat] * igain[...][None] + jnp.where(row_of == ONE, ishift[...][None], 0.0)
     r.mt[...] = jnp.zeros_like(r.mt)
     r.mt[:, :feat] = code
     code_high, code_low = split(code)
     code_both = jnp.concatenate([code_high, code_low], axis=0)
     for table, base in ((r.tk, 0), (r.tv, width)):
         for j in range(0, width, 256):
-            both = dot_nn(code_both, kvw[:, base + j : base + j + 256])
+            both = dot_nn(code_both, r.kvw[:, base + j : base + j + 256])
             high, low = split(both[:LANES] + both[LANES:])
             table[:LANES, j : j + 256] = high
             table[LANES : 2 * LANES, j : j + 256] = low
@@ -282,15 +384,15 @@
     r.ee[:LANES, :] = grid_code
     r.ee[LANES:, :] = grid_code
 
-    weights[0].wait()
+    WQ.wait()
     for j in range(0, width, 256):
         r.q[:, j : j + 256] = dot_nn(r.nl[...], r.wq[:, j : j + 256]).astype(BF16)
     query_code = dot_nt(r.q[...], r.tk[: 2 * LANES, :])
     query_code = (query_code[:, :LANES] + query_code[:, LANES:]) * scale
 
-    weights[1].wait()
-    for j in range(0, width, 256):
-        r.ag[:, j : j + 256] = dot_nt(cot[0], r.wd[j : j + 256, :])
+    WD.wait()
+    for j in range(0, width, 256):
+        r.ag[:, j : j + 256] = dot_nt(r.cot[...], r.wd[j : j + 256, :])
 
     counts_row = cnt[...].astype(F32)
     number = lax.broadcasted_iota(jnp.int32, (img, n_img), 0)
@@ -329,9 +431,9 @@
         rows_of = dot_nn(r.sel[...], r.pb[channel])
         window = jnp.concatenate([rows_of[j * img : (j + 1) * img] for j in range(9)], axis=1)
         for bit in range(7):
-            step = 1 << bit
-            moved = pltpu.roll(window, span - step, 1)
-            window = jnp.where((shift_of & step) != 0, moved, window)
+            hop = 1 << bit
+            moved = pltpu.roll(window, span - hop, 1)
+            window = jnp.where((shift_of & hop) != 0, moved, window)
         r.xi[channel] = jnp.where(inside, window[:, :CELLS], 0.0).astype(BF16)
 
     def gram_row(channel, x):
@@ -392,9 +494,9 @@
         r.merged[:, j : j + 256] = dot_nn(code_three, r.tv[:, j : j + 256]).astype(BF16)
     value_code_low = code_high
 
-    weights[2].wait()
-    for j in range(0, width, 256):
-        r.res[:, j : j + 256] = lat[0, :, j : j + 256].astype(F32) + dot_nn(r.merged[...], r.wo[:, j : j + 256])
+    WO.wait()
+    for j in range(0, width, 256):
+        r.res[:, j : j + 256] = r.lat[:, j : j + 256].astype(F32) + dot_nn(r.merged[...], r.wo[:, j : j + 256])
 
     def norm_mid(at):
         x = r.res[at, :]
@@ -406,7 +508,7 @@
         r.nm[at, :] = (hat * mgain[...] + mshift[...]).astype(BF16)
 
     by_rows(norm_mid)
-    weights[3].wait()
+    WU.wait()
     for j in range(0, width, 256):
         pre = dot_nn(r.nm[...], r.wu[:, j : j + 256])
         phi = 0.5 * (1.0 + lax.erf(pre * math.sqrt(0.5)))
@@ -422,10 +524,14 @@
     send_left(OUT)
 
     for j in range(0, width, 256):
-        o_mixed[0, :, j : j + 256] = (r.res[:, j : j + 256] + dot_nn(r.act[...], r.wd[:, j : j + 256])).astype(BF16)
+        r.nm[:, j : j + 256] = (r.res[:, j : j + 256] + dot_nn(r.act[...], r.wd[:, j : j + 256])).astype(BF16)
+    leave(r.nm, o_mixed.at[0])
+    product(DOWN)
+    start(DOWN, 0)
     for j in range(0, width, 256):
         r.ag[:, j : j + 256] = dot_nt(r.bt[UP, mine, :], r.wu[j : j + 256, :])
-    r.ar[0] = jnp.zeros_like(r.ar[0])
+    product(UP)
+    start(UP, 0)
     zero = jnp.zeros((1, width), F32)
 
     def norm_back(grad, hat, inv, gain):
@@ -435,18 +541,21 @@
     def mid_back(i, carry):
         at = pl.ds(pl.multiple_of(i * tile, tile), tile)
         grad, hat = r.ag[at, :], r.xm[at, :]
-        total = cot[0, at, :].astype(F32) + norm_back(grad, hat, r.rm[at, :1], mgain[...])
+        total = r.cot[at, :].astype(F32) + norm_back(grad, hat, r.rm[at, :1], mgain[...])
         r.res[at, :] = total
         r.bt[OUT, pl.ds(pl.multiple_of(c * LANES + i * tile, tile), tile), :] = total.astype(BF16)
         return carry[0] + jnp.sum(grad * hat, axis=0, keepdims=True), carry[1] + jnp.sum(grad, axis=0, keepdims=True)
 
     gain_sum, shift_sum = lax.fori_loop(0, LANES // tile, mid_back, (zero, zero))
-    r.ar[0, 2:3, :] = gain_sum
-    r.ar[0, 3:4, :] = shift_sum
+    r.vec[...] = jnp.zeros_like(r.vec)
+    r.vec[2:3, :] = gain_sum
+    r.vec[3:4, :] = shift_sum
     send_right(OUT)
     for j in range(0, width, 256):
         r.da[:, j : j + 256] = dot_nt(r.bt[OUT, mine, :], r.wo[j : j + 256, :]).astype(BF16)
 
+    product(OUT)
+    start(OUT, 0)
     back_code = dot_nt(r.da[...], r.tv[: 2 * LANES, :])
     back_code = back_code[:, :LANES] + back_code[:, LANES:]
     r.ag[...] = dot_nn(over_grid(back_code), r.ee[...])
@@ -479,14 +588,62 @@
         r.bt[QUERY, mine, j : j + 256] = dot_nn(code_three, r.tk[:, j : j + 256]).astype(BF16)
     send_right(QUERY)
 
-    for j in range(0, width, 256):
-        r.zt[j : j + 256, :] = dot_tn(r.q[:, j : j + 256], code_high).astype(BF16)
-        r.zt[width + j : width + j + 256, :] = dot_tn(r.da[:, j : j + 256], value_code_low).astype(BF16)
-    r.zc[...] = r.zt[...].reshape(r.zc.shape)
-    if parts["c"] > 1:
-        to_core("z", 8, r.zc.at[:, :, :, 1 - c], r.zcr)
-    else:
-        to_core("z", 8, r.zc.at[:, :, :, 0], r.zcr)
+    step(DOWN, 0)
+
+    for j in range(0, width, 256):
+        r.ag[:, j : j + 256] = dot_nt(r.bt[QUERY, mine, :], r.wq[j : j + 256, :])
+
+    def latents_back(i, carry):
+        at = pl.ds(pl.multiple_of(i * tile, tile), tile)
+        grad, hat = r.ag[at, :], r.xl[at, :]
+        r.res[at, :] = r.res[at, :] + norm_back(grad, hat, r.rl[at, :1], qgain[...])
+        return carry[0] + jnp.sum(grad * hat, axis=0, keepdims=True), carry[1] + jnp.sum(grad, axis=0, keepdims=True)
+
+    gain_sum, shift_sum = lax.fori_loop(0, LANES // tile, latents_back, (zero, zero))
+    r.vec[0:1, :] = gain_sum
+    r.vec[1:2, :] = shift_sum
+    leave(r.res, o_lat.at[0])
+    product(QUERY)
+    start(QUERY, 0)
+
+    heap = 256 // (2 * rows * parts["c"])
+    for j in range(0, 2 * width, 256):
+        if j < width:
+            made = dot_tn(r.q[:, j : j + 256], code_high)
+        else:
+            made = dot_tn(r.da[:, j - width : j - width + 256], value_code_low)
+        riding = pltpu.roll(r.vec[:, j // 2 : j // 2 + LANES].T, ONE + 1, 1).reshape(-1, rows, LANES)
+        made = made.reshape(-1, 2 * rows, LANES)
+        made = jnp.concatenate([made[:, :rows] + riding, made[:, rows:]], axis=1)
+        r.zc[heap * (j // 256) : heap * (j // 256 + 1)] = made.astype(BF16).reshape(heap, parts["c"], 2 * rows, LANES)
+    to_core("z", 8, r.zc.at[:, part("c", 1 - c)], r.zcr)
+    step(UP, 0)
+
+    in_gain, in_shift = jnp.zeros((feat, 1), F32), jnp.zeros((feat, 1), F32)
+    for j in range(0, 2 * width, 256):
+        sums = r.zc[heap * (j // 256) : heap * (j // 256 + 1)].reshape(256, LANES)
+        spread = dot_nt(r.fct[...], jnp.concatenate([sums, sums], axis=1))
+        factor = r.kvw[:, j : j + 256].astype(F32)
+        in_gain = in_gain + jnp.sum(factor * spread[:feat], axis=1, keepdims=True)
+        in_shift = in_shift + jnp.sum(factor * spread[wide : wide + 1], axis=1, keepdims=True)
+    for at, column in ((0, in_gain), (1, in_shift)):
+        for j in range(0, feat, LANES):
+            tall = min(LANES, feat - j)
+            eye = lax.broadcasted_iota(jnp.int32, (tall, LANES), 0) == lax.broadcasted_iota(jnp.int32, (tall, LANES), 1)
+            r.ar[0, at : at + 1, j : j + LANES] = jnp.sum(jnp.where(eye, column[j : j + tall], 0.0), axis=0, keepdims=True)
+    seq_copies = []
+    for offset in range(1, n_seq):
+        slot = n_seq - offset - 1
+        copy = pltpu.make_async_remote_copy(
+            src_ref=r.ar.at[0], dst_ref=r.ars.at[slot], send_sem=r.as_s.at[offset - 1], recv_sem=r.as_r.at[slot],
+            device_id=(z, lax.rem(s + offset, n_seq)), device_id_type=MESH,
+        )
+        copy.start()
+        seq_copies.append(copy)
+    core_copies.pop("z").wait()
+    both = r.zc[:, part("c", c)].astype(F32) + r.zcr[...].astype(F32)
+    r.zs0[0] = both.astype(BF16).reshape(parts["z"], parts["a"], parts["b"], 2 * rows, LANES)
+    start(SUMS, 0)
 
     query_t, back_t = query_code.T, back_code.T
     lifted = jnp.concatenate(
@@ -505,9 +662,9 @@
         own_grad = inv * steep - cube * gram_row(channel, colors)[1]
         window = jnp.concatenate([own_grad, jnp.zeros((img, LANES), F32)], axis=1)
         for bit in range(7):
-            step = 1 << bit
-            moved = pltpu.roll(window, step, 1)
-            window = jnp.where((shift_of & step) != 0, moved, window)
+            hop = 1 << bit
+            moved = pltpu.roll(window, hop, 1)
+            window = jnp.where((shift_of & hop) != 0, moved, window)
         for j in range(9):
             r.pg[j * img : (j + 1) * img, :] = window[:, j * LANES : (j + 1) * LANES]
         grad_high, grad_low = split(r.pg[...])
@@ -524,195 +681,72 @@
         copy.start()
         grad_copies.append(copy)
 
-    in_gain, in_shift = jnp.zeros((feat, 1), F32), jnp.zeros((feat, 1), F32)
-    for j in range(0, 2 * width, 256):
-        sums = r.zt[j : j + 256, :]
-        spread = dot_nt(fct[...], jnp.concatenate([sums, sums], axis=1))
-        factor = kvw[:, j : j + 256].astype(F32)
-        in_gain = in_gain + jnp.sum(factor * spread[:feat], axis=1, keepdims=True)
-        in_shift = in_shift + jnp.sum(factor * spread[wide : wide + 1], axis=1, keepdims=True)
-    for at, column in ((4, in_gain), (5, in_shift)):
-        for j in range(0, feat, LANES):
-            tall = min(LANES, feat - j)
-            eye = lax.broadcasted_iota(jnp.int32, (tall, LANES), 0) == lax.broadcasted_iota(jnp.int32, (tall, LANES), 1)
-            r.ar[0, at : at + 1, j : j + LANES] = jnp.sum(jnp.where(eye, column[j : j + tall], 0.0), axis=0, keepdims=True)
-
-    for j in range(0, width, 256):
-        r.ag[:, j : j + 256] = dot_nt(r.bt[QUERY, mine, :], r.wq[j : j + 256, :])
-
-    def latents_back(i, carry):
-        at = pl.ds(pl.multiple_of(i * tile, tile), tile)
-        grad, hat = r.ag[at, :], r.xl[at, :]
-        o_lat[0, at, :] = r.res[at, :] + norm_back(grad, hat, r.rl[at, :1], qgain[...])
-        return carry[0] + jnp.sum(grad * hat, axis=0, keepdims=True), carry[1] + jnp.sum(grad, axis=0, keepdims=True)
-
-    gain_sum, shift_sum = lax.fori_loop(0, LANES // tile, latents_back, (zero, zero))
-    r.ar[0, 0:1, :] = gain_sum
-    r.ar[0, 1:2, :] = shift_sum
-
-    def start_stage(key, stage, name, src_of, dst):
-        mat, half = key
-        copies = []
-        for offset in range(1, sizes[name]):
-            target = peer(name, offset)
-            slot = sizes[name] - offset - 1
-            copy = pltpu.make_async_remote_copy(
-                src_ref=src_of(part(name, target)), dst_ref=dst.at[slot],
-                send_sem=r.rs_s.at[mat, half, stage, offset - 1], recv_sem=r.rs_r.at[mat, half, stage, slot],
-                device_id=device(**{name: target}), device_id_type=MESH,
-            )
-            copy.start()
-            copies.append(copy)
-        return copies
-
-    def wait_all(copies):
-        for copy in copies:
-            copy.wait()
-
-    def gathered(own, dst, n):
-        total = own.astype(F32)
-        for slot in range(n - 1):
-            total = total + dst[slot].astype(F32)
-        return total
-
-    flying = {}
-
-    def buffers_of(mat):
-        return (r.zs0, r.zr, 0) if mat == 4 else (r.ms0, r.mr, mat)
-
-    def cut(mat, half):
-        if mat == 4:
-            return pl.ds(half * rows, rows), slice(None)
-        return slice(None), pl.ds(half * (width // 2), width // 2)
-
-    def blocks_at(mat, half, stage, target=None):
-        s0, received, i = buffers_of(mat)
-        at = {"z": slice(None), "a": slice(None), "b": slice(None)}
-        path = orders[half] + ("z",)
-        for done in path[:stage]:
-            at[done] = part(done, here[done])
-        at[path[stage]] = part(path[stage], here[path[stage]]) if target is None else target
-        return (i, at["z"], at["a"], at["b"]) + cut(mat, half)
-
-    def start(mat, stage):
-        s0, received, i = buffers_of(mat)
-        for half in range(2):
-            name = (orders[half] + ("z",))[stage]
-            flying[mat, half] = start_stage(
-                (mat, half), stage, name,
-                lambda p: s0.at[blocks_at(mat, half, stage, p)],
-                received[half][stage].at[i],
-            )
-
-    def step(mat, stage):
-        s0, received, i = buffers_of(mat)
-        for half in range(2):
-            wait_all(flying[mat, half])
-            name = (orders[half] + ("z",))[stage]
-            keep = blocks_at(mat, half, stage)
-            total = gathered(s0[keep], received[half][stage].at[i], sizes[name])
-            if stage < 2:
-                s0[keep] = total.astype(BF16)
-            elif mat == 4:
-                r.zout[cut(mat, half)] = total
-            else:
-                r.out[(mat,) + cut(mat, half)] = total
-        if stage < 2:
-            start(mat, stage + 1)
-
-    def product(mat):
-        core_copies.pop(("left", mat)).wait()
-        core_copies.pop(("right", mat)).wait()
-        left = r.at[mat, :, part("c", c)].reshape(-1, 2 * LANES)
-        for j in range(0, width, 256):
-            made = dot_nn(left, r.bt[mat, :, j : j + 256]).astype(BF16)
-            r.ms0[mat, :, :, :, :, j : j + 256] = made.reshape(parts["z"], parts["a"], parts["b"], rows, 256)
-
-    for mat in range(4):
-        product(mat)
-        start(mat, 0)
-    core_copies.pop("z").wait()
-    r.zs0[0] = (r.zc[:, :, :, part("c", c)].astype(F32) + r.zcr[...].astype(F32)).astype(BF16)
-    start(4, 0)
-
-    small = {}
-
-    def small_start(stage):
-        name = SMALL_ORDER[stage]
-        copies = []
-        for offset in range(1, sizes[name]):
-            slot = sizes[name] - offset - 1
-            copy = pltpu.make_async_remote_copy(
-                src_ref=r.ar.at[stage], dst_ref=r.arr[stage].at[slot],
-                send_sem=r.ar_s.at[stage, offset - 1], recv_sem=r.ar_r.at[stage, slot],
-                device_id=device(**{name: peer(name, offset)}), device_id_type=MESH,
-            )
-            copy.start()
-            copies.append(copy)
-        small[stage] = copies
-
-    def small_end(stage):
-        name = SMALL_ORDER[stage]
-        wait_all(small[stage])
-        total = r.ar[stage]
-        for slot in range(sizes[name] - 1):
-            total = total + r.arr[stage][slot]
-        r.ar[stage + 1] = total
-
-    small_start(0)
-    small_end(0)
-    small_start(1)
-    step(0, 0)
-    small_end(1)
-    small_start(2)
-    step(1, 0)
-    small_end(2)
-    small_start(3)
-    step(0, 1)
-    step(2, 0)
-    step(1, 1)
-    step(3, 0)
-    step(2, 1)
-    step(4, 0)
-    small_end(3)
-    for copy in grad_copies:
-        copy.wait()
-    pixel = r.pgs[:, own, :]
-    for slot in range(n_seq - 1):
-        pixel = pixel + r.pgr[slot]
-    for channel in range(3):
-        for j in range(blocks):
-            o_pix[0, channel : channel + 1, j * LANES : (j + 1) * LANES] = pixel[channel, j : j + 1, :]
-    step(0, 2)
-    step(1, 2)
-    step(3, 1)
-    step(4, 1)
-    step(2, 2)
-    step(3, 2)
-    step(4, 2)
+    step(DOWN, 1)
+    step(OUT, 0)
+    step(UP, 1)
+    wait_all(seq_copies)
+    r.ar[1] = gathered(r.ar[0], r.ars, n_seq)
+    z_copies = []
+    for offset in range(1, n_batch):
+        slot = n_batch - offset - 1
+        copy = pltpu.make_async_remote_copy(
+            src_ref=r.ar.at[1], dst_ref=r.arz.at[slot], send_sem=r.az_s.at[offset - 1], recv_sem=r.az_r.at[slot],
+            device_id=(peer("z", offset), s), device_id_type=MESH,
+        )
+        copy.start()
+        z_copies.append(copy)
+    step(QUERY, 0)
+    step(OUT, 1)
+    step(SUMS, 0)
 
     total_rows = width // (n_batch * n_seq)
     inner = 0
     for name in ("a", "b", "c"):
         if parts[name] < sizes[name]:
             inner = inner * sizes[name] + here[name]
-    for mat, made in enumerate((o_wd, o_wu, o_wo, o_wq)):
-        if total_rows == rows:
-            made[...] = r.out[mat]
-        else:
-            made[...] = pltpu.roll(r.out[mat], lax.rem(rows - inner * total_rows, rows), 0)[:total_rows]
-    index = z * n_seq + s
-    turned = pltpu.roll(r.ar[4], lax.rem(width - index * total_rows, width), 1)
-    o_vec[...] = turned[:4, :total_rows]
-    o_in[...] = r.ar[4, 4:6, :feat]
+
+    def finish(mat, made):
+        step(mat, 2)
+        if total_rows < rows:
+            r.out[mat] = pltpu.roll(r.out[mat], lax.rem(rows - inner * total_rows, rows), 0)
+        leave(r.out.at[mat, :total_rows], made)
+
+    finish(DOWN, o_wd)
+    step(QUERY, 1)
+    step(SUMS, 1)
+    wait_all(grad_copies)
+    o_pix[...] = gathered(r.pgs[:, own, :], r.pgr, n_seq)
+    finish(UP, o_wu)
+    wait_all(z_copies)
+    o_in[...] = gathered(r.ar[1], r.arz, n_batch)[:, :feat]
+    finish(OUT, o_wo)
+    finish(QUERY, o_wq)
+    step(SUMS, 2)
+    sums = r.zout[...]
+    turned = sums
+    if total_rows < rows:
+        turned = pltpu.roll(sums, lax.rem(rows - inner * total_rows, rows), 0)
+        sums = pltpu.roll(sums, lax.rem(2 * (rows - inner * total_rows), 2 * rows), 0)
+    high, low = split(sums)
     code_high, code_low = split(r.mt[...].T)
     spread_left = jnp.concatenate([code_high, code_high, code_low], axis=1)
-    if total_rows == rows:
-        sums = r.zout[...]
-    else:
-        sums = pltpu.roll(r.zout[...], lax.rem(2 * (rows - inner * total_rows), 2 * rows), 0)[: 2 * total_rows]
-    high, low = split(sums)
-    o_kv[...] = dot_nt(spread_left, jnp.concatenate([high, low, high], axis=1))[:feat]
+    o_kv[...] = dot_nt(jnp.concatenate([high, low, high], axis=1), spread_left)[: 2 * total_rows, :feat]
+    square = jnp.concatenate([turned, jnp.zeros((LANES - 2 * rows, LANES), F32)], axis=0)
+    o_vec[...] = square.T[COLOR : COLOR + 8, :total_rows]
+    wait_all(leaving)
+
+
+def hand_over(mixed, lat, pix, vec, wq, inner, kv, wo, wu, wd, *refs):
+    o_mixed, o_lat, o_pix, o_qg, o_qs, o_wq, o_ig, o_is, o_kv, o_wo, o_mg, o_ms, o_wu, o_wd = refs
+    for src, dst in ((mixed, o_mixed), (lat, o_lat), (wq, o_wq), (wo, o_wo), (wu, o_wu), (wd, o_wd), (kv, o_kv)):
+        dst[...] = src[...]
+    for channel in range(3):
+        for j in range(pix.shape[1]):
+            o_pix[channel, 0:1, j * LANES : (j + 1) * LANES] = pix[channel, j : j + 1, :]
+    for i, dst in enumerate((o_qg, o_qs, o_mg, o_ms)):
+        dst[...] = vec[4 + i, :]
+    for i, dst in enumerate((o_ig, o_is)):
+        dst[...] = inner[i, :]
 
 
 def solution(mesh):
@@ -729,40 +763,42 @@
         rows = width // (n_batch * n_seq)
         vm = pl.BlockSpec(memory_space=pltpu.VMEM)
         hbm = pl.BlockSpec(memory_space=pl.ANY)
-        out_shape = (
-            jax.ShapeDtypeStruct(latents.shape, BF16),
-            jax.ShapeDtypeStruct(latents.shape, F32),
-            jax.ShapeDtypeStruct(pixels.shape, F32),
-            jax.ShapeDtypeStruct((4, rows), F32),
-            jax.ShapeDtypeStruct((rows, width), F32),
-            jax.ShapeDtypeStruct((2, feat), F32),
-            jax.ShapeDtypeStruct((feat, 2 * rows), F32),
-            jax.ShapeDtypeStruct((rows, width), F32),
-            jax.ShapeDtypeStruct((rows, width), F32),
-            jax.ShapeDtypeStruct((rows, width), F32),
-        )
+        f32 = lambda *shape: jax.ShapeDtypeStruct(shape, F32)
+        mixed, latent_grad, square = jax.ShapeDtypeStruct(latents.shape, BF16), f32(*latents.shape), f32(rows, width)
+        kv = f32(2 * rows, feat)
         args = (
-            latents, pixels.reshape(3, pix_dev // LANES, LANES), counts, latent_image,
-            query_gain[None], query_shift[None], query_weight, input_gain[None], input_shift[None], kv_weight,
+            latents, pixels, counts, latent_image,
+            query_gain[None], query_shift[None], query_weight, input_gain, input_shift, kv_weight,
             out_weight, mlp_gain[None], mlp_shift[None], up_weight, down_weight, cotangent,
             jnp.asarray(fc), jnp.asarray(geo), jnp.asarray(fct),
         )
+        in_hbm = (0, 6, 9, 10, 13, 14, 15, 16, 18)
+        big = (0, 1, 4, 7, 8, 9)
         made = pl.pallas_call(
             functools.partial(layer, n_batch, n_seq, width, n_img, feat, gram),
-            out_shape=out_shape,
-            in_specs=[hbm if getattr(arg, "shape", ()) == (width, width) else vm for arg in args],
-            out_specs=[vm] * len(out_shape),
+            out_shape=(
+                mixed, latent_grad, f32(3, pix_dev // LANES, LANES), f32(8, rows), square, f32(2, feat), kv, square, square, square,
+            ),
+            in_specs=[hbm if i in in_hbm else vm for i in range(len(args))],
+            out_specs=[hbm if i in big else vm for i in range(10)],
             scratch_shapes=[vars(scratch)],
             compiler_params=pltpu.CompilerParams(
                 collective_id=0, has_side_effects=True, vmem_limit_bytes=60 * 1024 * 1024
             ),
             name="layer",
         )(*args)
-        mixed, latent_grad, pixel_grad, vectors, wq, inner, kv, wo, wu, wd = made
-        return (
-            mixed, latent_grad, pixel_grad, vectors[0], vectors[1], wq, inner[0], inner[1], kv, wo,
-            vectors[2], vectors[3], wu, wd,
+        out_shape = (
+            mixed, latent_grad, f32(3, 1, pix_dev), f32(rows), f32(rows), square, f32(feat), f32(feat), kv, square,
+            f32(rows), f32(rows), square, square,
         )
+        out = pl.pallas_call(
+            hand_over,
+            out_shape=out_shape,
+            in_specs=[vm] * len(made),
+            out_specs=[vm] * len(out_shape),
+            name="hand_over",
+        )(*made)
+        return (*out[:2], out[2].transpose(1, 0, 2), *out[3:8], out[8].T, *out[9:])
 
     whole, vec = P(("batch", "seq"), None), P(("batch", "seq"))
     rowed = P("batch", "seq", None)

time: 109 us -> 78 us (0.72)
  local copies, waits for them, and re-layouts: 16.6 us -> 0 us
  Pallas kernels: 91.5 us -> 77 us
    pallas_call x1, Pallas kernels: 91.5 us -> 74.5 us  [body(): pl.pallas_call(functools.partial(layer, n_batch, n_seq, width, n_img, fea...]
    unnamed x15 -> x0, local copies, waits for them, and re-layouts: 11.5 us -> none
    broadcast_in_dim x2 -> x0, local copies, waits for them, and re-layouts: 2.49 us -> none  [the longest x1 1.25 us: body(): input_gain[None]]
    pallas_call x0 -> x1, Pallas kernels: none -> 2.46 us  [body(): pl.pallas_call(hand_over, out_shape=out_shape, in_specs=[vm] * len(made),...]
    slice x1 -> x0, local copies, waits for them, and re-layouts: 1.34 us -> none  [body(): inner[1]]
    squeeze x1 -> x0, local copies, waits for them, and re-layouts: 1.33 us -> none  [body(): vectors[3]]
where the time goes in v2:
time: 78 us; the launch traced here: 77.8 us
  Pallas kernels  77 us (99%)
  between operations  0.82 us (1%)
    pallas_call x1, Pallas kernels, body(): pl.pallas_call(functools.partial(layer, n_batch, n_seq, width, n_img, fea...  74.5 us
    pallas_call x1, Pallas kernels, body(): pl.pallas_call(hand_over, out_shape=out_shape, in_specs=[vm] * len(made),...  2.46 us

profile of v2, /device:TPU:0, one launch (start us, length us, event | category | flops | bytes accessed | tf_op | source)
XLA Modules:
  0.0 77.8 jit_solution(8890515538085134689)
XLA Ops:
  0.7 74.5 %layer.1 = (bf16[1,128,1024]{2,1,0:T(8,128)(2,1)}, f32[1,128,1024]{2,1,0:T(8,128)}, f32[3,16,128]{2,1,0:T(8,128)}, f32[8,32]{1,0:T(8,128)}, f32[32,1024]{1,0:T(8...) custom-call(bf16[1,128,1024]{2,1,0:T(8,128)(2,1)} %h_lat.1, ...), custom_call_target="tpu_custom_call" | custom-call | tf_op jit(solution)/shard_map/layer/pallas_call | solution.py:777
  75.2 2.5 %hand_over.1 = (bf16[1,128,1024]{2,1,0:T(8,128)(2,1)}, f32[1,128,1024]{2,1,0:T(8,128)}, f32[3,1,2048]{2,1,0:T(1,128)}, f32[32]{0:T(128)}, f32[32]{0:T(128)}, /*i...) custom-call(bf16[1,128,1024]{2,1,0:T(8,128)(2,1)} %get-tuple-element, ...), custom_call_target="tpu_custom_call" | custom-call | tf_op jit(solution)/shard_map/hand_over/pallas_call | solution.py:794

commit v3 on v2

--- a/solution.py
+++ b/solution.py
@@ -86,6 +86,10 @@
             parts[name] = 1
     orders = (("b", "a") if parts["b"] > 1 else ("a", "b"), ("a", "b"))
     return sizes, parts, width // math.prod(parts.values()), orders
+
+
+def by_columns(n_seq, width):
+    return width // n_seq % LANES == 0
 
 
 def shapes_of(n_batch, n_seq, width, pix_dev, n_img, feat):
@@ -121,18 +125,29 @@
     S.pg = vm(9 * img, LANES, dtype=F32)
     S.pgs = vm(3, n_seq * blocks, LANES, dtype=F32)
     S.pgr = vm(n_seq - 1, 3, blocks, LANES, dtype=F32)
-    S.at = vm(4, *factor_rows, 2 * LANES)
-    S.bt = vm(4, 2 * LANES, width)
-    S.ms0 = vm(4, parts["z"], parts["a"], parts["b"], rows, width)
+    tall, plane, apart = width // n_batch, n_seq // 2, by_columns(n_seq, width)
+    full = 2 if apart else 3
+    S.at = vm(full, *factor_rows, 2 * LANES)
+    S.bt = vm(3, 2 * LANES, width)
+    S.ms0 = vm(full, parts["z"], parts["a"], parts["b"], rows, width)
+    S.ds0 = vm(1, 1, parts["a"], parts["b"], rows, width)
     S.zs0 = vm(1, parts["z"], parts["a"], parts["b"], 2 * rows, LANES)
-    S.mr, S.zr = [], []
-    for made, mats, across in ((S.mr, 4, width // 2), (S.zr, 1, LANES)):
+    S.mr, S.dr, S.zr = [], [], []
+    for made, mats, deep, across in ((S.mr, full, parts["z"], width // 2), (S.dr, 1, 1, width // 2), (S.zr, 1, parts["z"], LANES)):
         for first, other in orders:
             made.append([
-                vm(mats, sizes[first] - 1, parts["z"], parts[other], rows, across),
-                vm(mats, sizes[other] - 1, parts["z"], rows, across),
-                vm(mats, sizes["z"] - 1, rows, across),
-            ])
+                vm(mats, sizes[first] - 1, deep, parts[other], rows, across),
+                vm(mats, sizes[other] - 1, deep, rows, across),
+            ] + [vm(mats, sizes["z"] - 1, rows, across)] * (deep > 1))
+    S.gz, S.az = vm(n_batch * LANES, width), vm(n_batch * LANES, tall)
+    S.dc = vm(parts["a"], parts["b"], parts["c"], rows, width)
+    S.dcr = vm(parts["a"], parts["b"], rows, width)
+    if apart:
+        S.np, S.qp = vm(plane * LANES, width), vm(plane * LANES, width // plane)
+        S.qc, S.qcr = vm(2, width // n_seq, width), vm(width // n_seq, width)
+        S.qz = vm(n_batch - 1, width // n_seq, tall)
+        S.qt = vm(tall, width // n_seq, dtype=F32)
+        S.qo = vm(tall // n_seq, width, dtype=F32)
     S.zc = vm(width // (rows * parts["c"]), parts["c"], 2 * rows, LANES)
     S.zcr = vm(width // (rows * parts["c"]), 2 * rows, LANES)
     S.vec = vm(LANES, width, dtype=F32)
@@ -152,9 +167,12 @@
     S.px_s, S.px_r = sem(n_seq - 1), sem(n_seq - 1)
     S.pg_s, S.pg_r = sem(n_seq - 1), sem(n_seq - 1)
     S.co_s, S.co_r = sem(9), sem(9)
+    S.gz_s, S.gz_r, S.az_s, S.az_r, S.qz_s, S.qz_r = [sem(n_batch - 1)] * 6
+    S.np_s, S.np_r, S.qp_s, S.qp_r = [sem(plane - 1)] * 4
+    S.qo_s, S.qo_r = [sem(n_seq - 1)] * 2
     S.rs_s, S.rs_r = sem(5, 2, 3, most), sem(5, 2, 3, most)
     S.as_s, S.as_r = sem(n_seq - 1), sem(n_seq - 1)
-    S.az_s, S.az_r = sem(n_batch - 1), sem(n_batch - 1)
+    S.ab_s, S.ab_r = sem(n_batch - 1), sem(n_batch - 1)
     return S
 
 
@@ -210,6 +228,9 @@
         copy.start()
         leaving.append(copy)
 
+    UP, OUT, QUERY, DOWN, SUMS = range(5)
+    apart = by_columns(n_seq, width)
+    tall, plane = width // n_batch, n_seq // 2
     tile = 16
 
     def by_rows(step):
@@ -276,10 +297,12 @@
     flying = {}
 
     def buffers_of(mat):
-        return (r.zs0, r.zr, 0) if mat == 4 else (r.ms0, r.mr, mat)
+        if mat == DOWN:
+            return r.ds0, r.dr, 0
+        return (r.zs0, r.zr, 0) if mat == SUMS else (r.ms0, r.mr, mat)
 
     def cut(mat, half):
-        if mat == 4:
+        if mat == SUMS:
             return pl.ds(half * rows, rows), slice(None)
         return slice(None), pl.ds(half * (width // 2), width // 2)
 
@@ -304,19 +327,40 @@
 
     def step(mat, stage):
         s0, received, i = buffers_of(mat)
+        last = 1 if mat == DOWN else 2
         for half in range(2):
             wait_all(flying[mat, half])
             name = (orders[half] + ("z",))[stage]
             keep = blocks_at(mat, half, stage)
             total = gathered(s0[keep], received[half][stage].at[i], sizes[name])
-            if stage < 2:
+            if stage < last:
                 s0[keep] = total.astype(BF16)
-            elif mat == 4:
+            elif mat == SUMS:
                 r.zout[cut(mat, half)] = total
             else:
-                r.out[(mat,) + cut(mat, half)] = total
-        if stage < 2:
+                r.out[(mat,) + cut(mat, half)] = total[0] if mat == DOWN else total
+        if stage < last:
             start(mat, stage + 1)
+
+    def exchange(n, index, device_at, src_of, dst, sends, receives):
+        copies = []
+        for offset in range(1, n):
+            target = lax.rem(index + offset, n)
+            copy = pltpu.make_async_remote_copy(
+                src_ref=src_of(target), dst_ref=dst(n - offset - 1), send_sem=sends.at[offset - 1],
+                recv_sem=receives.at[n - offset - 1], device_id=device_at(target), device_id_type=MESH,
+            )
+            copy.start()
+            copies.append(copy)
+        return copies
+
+    def span_of(index, size):
+        return pl.ds(pl.multiple_of(index * size, size), size)
+
+    on_z = lambda target: (target, s)
+    in_plane = lambda target: (z, target * 2 + c)
+    in_row = lambda target: (z, target)
+    spot = s // 2
 
     def product(mat):
         core_copies.pop(("left", mat)).wait()
@@ -336,11 +380,13 @@
         r.nl[at, :] = (hat * qgain[...] + qshift[...]).astype(BF16)
 
     LAT.wait()
-    DOWN, UP, OUT, QUERY, SUMS = range(5)
     by_rows(norm_latents)
-    turn(QUERY, r.nl)
     COT.wait()
-    r.bt[DOWN, mine, :] = r.cot[...]
+    r.gz[span_of(z, LANES), :] = r.cot[...]
+    if apart:
+        r.np[span_of(spot, LANES), :] = r.nl[...]
+    else:
+        turn(QUERY, r.nl)
 
     own = pl.ds(pl.multiple_of(s * blocks, blocks), blocks)
     colors = px[0].astype(F32)
@@ -358,8 +404,13 @@
         )
         copy.start()
         pixel_copies.append(copy)
-    send_left(QUERY)
-    send_right(DOWN)
+    if apart:
+        own_norm = r.np.at[span_of(spot, LANES), :]
+        norm_copies = exchange(plane, spot, in_plane, lambda target: own_norm, lambda slot: own_norm, r.np_s, r.np_r)
+    else:
+        send_left(QUERY)
+    own_cot = r.gz.at[span_of(z, LANES), :]
+    cot_copies = exchange(n_batch, z, on_z, lambda target: own_cot, lambda slot: own_cot, r.gz_s, r.gz_r)
 
     FCT.wait()
     FC.wait()
@@ -515,8 +566,11 @@
         r.act[:, j : j + 256] = (pre * phi).astype(BF16)
         slope = phi + pre * (jnp.exp(-0.5 * pre * pre) * (1.0 / math.sqrt(2.0 * math.pi)))
         r.bt[UP, mine, j : j + 256] = (r.ag[:, j : j + 256] * slope).astype(BF16)
-    turn(DOWN, r.act)
-    send_left(DOWN)
+    part_z = span_of(z, LANES)
+    act_copies = exchange(
+        n_batch, z, on_z, lambda target: r.act.at[:, span_of(target, tall)], lambda slot: r.az.at[part_z, :], r.az_s, r.az_r
+    )
+    r.az[part_z, :] = r.act[:, span_of(z, tall)]
     turn(UP, r.nm)
     send_left(UP)
     send_right(UP)
@@ -526,8 +580,6 @@
     for j in range(0, width, 256):
         r.nm[:, j : j + 256] = (r.res[:, j : j + 256] + dot_nn(r.act[...], r.wd[:, j : j + 256])).astype(BF16)
     leave(r.nm, o_mixed.at[0])
-    product(DOWN)
-    start(DOWN, 0)
     for j in range(0, width, 256):
         r.ag[:, j : j + 256] = dot_nt(r.bt[UP, mine, :], r.wu[j : j + 256, :])
     product(UP)
@@ -554,8 +606,6 @@
     for j in range(0, width, 256):
         r.da[:, j : j + 256] = dot_nt(r.bt[OUT, mine, :], r.wo[j : j + 256, :]).astype(BF16)
 
-    product(OUT)
-    start(OUT, 0)
     back_code = dot_nt(r.da[...], r.tv[: 2 * LANES, :])
     back_code = back_code[:, :LANES] + back_code[:, LANES:]
     r.ag[...] = dot_nn(over_grid(back_code), r.ee[...])
@@ -586,9 +636,19 @@
     code_three = jnp.concatenate([code_high, code_high, code_low], axis=1)
     for j in range(0, width, 256):
         r.bt[QUERY, mine, j : j + 256] = dot_nn(code_three, r.tk[:, j : j + 256]).astype(BF16)
-    send_right(QUERY)
-
-    step(DOWN, 0)
+    if apart:
+        part_p = span_of(spot, LANES)
+        piece = width // plane
+        query_copies = exchange(
+            plane, spot, in_plane, lambda target: r.bt.at[QUERY, mine, span_of(target, piece)], lambda slot: r.qp.at[part_p, :],
+            r.qp_s, r.qp_r,
+        )
+        r.qp[part_p, :] = r.bt[QUERY, mine, span_of(spot, piece)]
+    else:
+        send_right(QUERY)
+    product(OUT)
+    start(OUT, 0)
+    step(UP, 0)
 
     for j in range(0, width, 256):
         r.ag[:, j : j + 256] = dot_nt(r.bt[QUERY, mine, :], r.wq[j : j + 256, :])
@@ -603,8 +663,16 @@
     r.vec[0:1, :] = gain_sum
     r.vec[1:2, :] = shift_sum
     leave(r.res, o_lat.at[0])
-    product(QUERY)
-    start(QUERY, 0)
+    if apart:
+        wait_all(norm_copies)
+        wait_all(query_copies)
+        for j in range(0, width, 256):
+            made = dot_tn(r.qp[...], r.np[:, j : j + 256]).astype(BF16)
+            r.qc[:, :, j : j + 256] = made.reshape(2, width // n_seq, 256)
+        to_core("q", 6, r.qc.at[1 - c], r.qcr)
+    else:
+        product(QUERY)
+        start(QUERY, 0)
 
     heap = 256 // (2 * rows * parts["c"])
     for j in range(0, 2 * width, 256):
@@ -617,7 +685,18 @@
         made = jnp.concatenate([made[:, :rows] + riding, made[:, rows:]], axis=1)
         r.zc[heap * (j // 256) : heap * (j // 256 + 1)] = made.astype(BF16).reshape(heap, parts["c"], 2 * rows, LANES)
     to_core("z", 8, r.zc.at[:, part("c", 1 - c)], r.zcr)
-    step(UP, 0)
+    if apart:
+        core_copies.pop("q").wait()
+        r.qcr[...] = (r.qc[c].astype(F32) + r.qcr[...].astype(F32)).astype(BF16)
+        sum_copies = exchange(
+            n_batch, z, on_z, lambda target: r.qcr.at[:, span_of(target, tall)], lambda slot: r.qz.at[slot], r.qz_s, r.qz_r
+        )
+    wait_all(cot_copies)
+    wait_all(act_copies)
+    for j in range(0, width, 256):
+        made = dot_tn(r.az[...], r.gz[:, j : j + 256]).astype(BF16)
+        r.dc[:, :, :, :, j : j + 256] = made.reshape(parts["a"], parts["b"], parts["c"], rows, 256)
+    to_core("d", 7, r.dc.at[:, :, part("c", 1 - c)], r.dcr)
 
     in_gain, in_shift = jnp.zeros((feat, 1), F32), jnp.zeros((feat, 1), F32)
     for j in range(0, 2 * width, 256):
@@ -628,9 +707,9 @@
         in_shift = in_shift + jnp.sum(factor * spread[wide : wide + 1], axis=1, keepdims=True)
     for at, column in ((0, in_gain), (1, in_shift)):
         for j in range(0, feat, LANES):
-            tall = min(LANES, feat - j)
-            eye = lax.broadcasted_iota(jnp.int32, (tall, LANES), 0) == lax.broadcasted_iota(jnp.int32, (tall, LANES), 1)
-            r.ar[0, at : at + 1, j : j + LANES] = jnp.sum(jnp.where(eye, column[j : j + tall], 0.0), axis=0, keepdims=True)
+            some = min(LANES, feat - j)
+            eye = lax.broadcasted_iota(jnp.int32, (some, LANES), 0) == lax.broadcasted_iota(jnp.int32, (some, LANES), 1)
+            r.ar[0, at : at + 1, j : j + LANES] = jnp.sum(jnp.where(eye, column[j : j + some], 0.0), axis=0, keepdims=True)
     seq_copies = []
     for offset in range(1, n_seq):
         slot = n_seq - offset - 1
@@ -644,6 +723,9 @@
     both = r.zc[:, part("c", c)].astype(F32) + r.zcr[...].astype(F32)
     r.zs0[0] = both.astype(BF16).reshape(parts["z"], parts["a"], parts["b"], 2 * rows, LANES)
     start(SUMS, 0)
+    core_copies.pop("d").wait()
+    r.ds0[0, 0] = (r.dc[:, :, part("c", c)].astype(F32) + r.dcr[...].astype(F32)).astype(BF16)
+    start(DOWN, 0)
 
     query_t, back_t = query_code.T, back_code.T
     lifted = jnp.concatenate(
@@ -681,23 +763,30 @@
         copy.start()
         grad_copies.append(copy)
 
-    step(DOWN, 1)
+    step(UP, 1)
+    if apart:
+        wait_all(sum_copies)
+        made = gathered(r.qcr[:, span_of(z, tall)], r.qz, n_batch)
+        for j in range(0, tall, LANES):
+            r.qt[j : j + LANES, :] = made[:, j : j + LANES].T
+        few = tall // n_seq
+        part_q = r.qo.at[:, span_of(s, LANES)]
+        last_copies = exchange(
+            n_seq, s, in_row, lambda target: r.qt.at[span_of(target, few), :], lambda slot: part_q, r.qo_s, r.qo_r
+        )
+        r.qo[:, span_of(s, LANES)] = r.qt[span_of(s, few), :]
+    else:
+        step(QUERY, 0)
     step(OUT, 0)
-    step(UP, 1)
+    step(SUMS, 0)
+    step(DOWN, 0)
     wait_all(seq_copies)
     r.ar[1] = gathered(r.ar[0], r.ars, n_seq)
-    z_copies = []
-    for offset in range(1, n_batch):
-        slot = n_batch - offset - 1
-        copy = pltpu.make_async_remote_copy(
-            src_ref=r.ar.at[1], dst_ref=r.arz.at[slot], send_sem=r.az_s.at[offset - 1], recv_sem=r.az_r.at[slot],
-            device_id=(peer("z", offset), s), device_id_type=MESH,
-        )
-        copy.start()
-        z_copies.append(copy)
-    step(QUERY, 0)
+    z_copies = exchange(n_batch, z, on_z, lambda target: r.ar.at[1], lambda slot: r.arz.at[slot], r.ab_s, r.ab_r)
     step(OUT, 1)
-    step(SUMS, 0)
+    step(SUMS, 1)
+    if not apart:
+        step(QUERY, 1)
 
     total_rows = width // (n_batch * n_seq)
     inner = 0
@@ -706,21 +795,23 @@
             inner = inner * sizes[name] + here[name]
 
     def finish(mat, made):
-        step(mat, 2)
+        step(mat, 1 if mat == DOWN else 2)
         if total_rows < rows:
             r.out[mat] = pltpu.roll(r.out[mat], lax.rem(rows - inner * total_rows, rows), 0)
         leave(r.out.at[mat, :total_rows], made)
 
-    finish(DOWN, o_wd)
-    step(QUERY, 1)
-    step(SUMS, 1)
     wait_all(grad_copies)
     o_pix[...] = gathered(r.pgs[:, own, :], r.pgr, n_seq)
+    finish(DOWN, o_wd)
     finish(UP, o_wu)
+    if apart:
+        wait_all(last_copies)
+        leave(r.qo, o_wq)
+    else:
+        finish(QUERY, o_wq)
     wait_all(z_copies)
     o_in[...] = gathered(r.ar[1], r.arz, n_batch)[:, :feat]
     finish(OUT, o_wo)
-    finish(QUERY, o_wq)
     step(SUMS, 2)
     sums = r.zout[...]
     turned = sums

time: 78 us -> 67.3 us (0.86)
  Pallas kernels: 77 us -> 66.3 us
    pallas_call x1, Pallas kernels: 74.5 us -> 63.8 us  [body(): pl.pallas_call(functools.partial(layer, n_batch, n_seq, width, n_img, fea...]
where the time goes in v3:
time: 67.3 us; the launch traced here: 67.1 us
  Pallas kernels  66.3 us (99%)
  between operations  0.82 us (1%)
    pallas_call x1, Pallas kernels, body(): pl.pallas_call(functools.partial(layer, n_batch, n_seq, width, n_img, fea...  63.8 us
    pallas_call x1, Pallas kernels, body(): pl.pallas_call(hand_over, out_shape=out_shape, in_specs=[vm] * len(made),...  2.46 us

profile of v3, /device:TPU:0, one launch (start us, length us, event | category | flops | bytes accessed | tf_op | source)
XLA Modules:
  0.0 67.1 jit_solution(15089331356485142085)
XLA Ops:
  0.7 63.8 %layer.1 = (bf16[1,128,1024]{2,1,0:T(8,128)(2,1)}, f32[1,128,1024]{2,1,0:T(8,128)}, f32[3,16,128]{2,1,0:T(8,128)}, f32[8,32]{1,0:T(8,128)}, f32[32,1024]{1,0:T(8...) custom-call(bf16[1,128,1024]{2,1,0:T(8,128)(2,1)} %h_lat.1, ...), custom_call_target="tpu_custom_call" | custom-call | tf_op jit(solution)/shard_map/layer/pallas_call | solution.py:868
  64.5 2.5 %hand_over.1 = (bf16[1,128,1024]{2,1,0:T(8,128)(2,1)}, f32[1,128,1024]{2,1,0:T(8,128)}, f32[3,1,2048]{2,1,0:T(1,128)}, f32[32]{0:T(128)}, f32[32]{0:T(128)}, /*i...) custom-call(bf16[1,128,1024]{2,1,0:T(8,128)(2,1)} %get-tuple-element, ...), custom_call_target="tpu_custom_call" | custom-call | tf_op jit(solution)/shard_map/hand_over/pallas_call | solution.py:885

commit v4 on v3

--- a/solution.py
+++ b/solution.py
@@ -238,7 +238,7 @@
             step(pl.ds(pl.multiple_of(i * tile, tile), tile))
             return carry
 
-        lax.fori_loop(0, LANES // tile, run, 0)
+        lax.fori_loop(0, LANES // tile, run, 0, unroll=8)
 
     mine = pl.ds(pl.multiple_of(c * LANES, LANES), LANES)
 
@@ -598,7 +598,7 @@
         r.bt[OUT, pl.ds(pl.multiple_of(c * LANES + i * tile, tile), tile), :] = total.astype(BF16)
         return carry[0] + jnp.sum(grad * hat, axis=0, keepdims=True), carry[1] + jnp.sum(grad, axis=0, keepdims=True)
 
-    gain_sum, shift_sum = lax.fori_loop(0, LANES // tile, mid_back, (zero, zero))
+    gain_sum, shift_sum = lax.fori_loop(0, LANES // tile, mid_back, (zero, zero), unroll=8)
     r.vec[...] = jnp.zeros_like(r.vec)
     r.vec[2:3, :] = gain_sum
     r.vec[3:4, :] = shift_sum
@@ -646,146 +646,178 @@
         r.qp[part_p, :] = r.bt[QUERY, mine, span_of(spot, piece)]
     else:
         send_right(QUERY)
+    kept = SimpleNamespace()
+    heap = 256 // (2 * rows * parts["c"])
+
+    def latents_gradient():
+        for j in range(0, width, 256):
+            r.ag[:, j : j + 256] = dot_nt(r.bt[QUERY, mine, :], r.wq[j : j + 256, :])
+
+        def latents_back(i, carry):
+            at = pl.ds(pl.multiple_of(i * tile, tile), tile)
+            grad, hat = r.ag[at, :], r.xl[at, :]
+            r.res[at, :] = r.res[at, :] + norm_back(grad, hat, r.rl[at, :1], qgain[...])
+            return carry[0] + jnp.sum(grad * hat, axis=0, keepdims=True), carry[1] + jnp.sum(grad, axis=0, keepdims=True)
+
+        gain_sum, shift_sum = lax.fori_loop(0, LANES // tile, latents_back, (zero, zero), unroll=8)
+        r.vec[0:1, :] = gain_sum
+        r.vec[1:2, :] = shift_sum
+        leave(r.res, o_lat.at[0])
+
+    def query_product():
+        if apart:
+            wait_all(norm_copies)
+            wait_all(query_copies)
+            for j in range(0, width, 256):
+                made = dot_tn(r.qp[...], r.np[:, j : j + 256]).astype(BF16)
+                r.qc[:, :, j : j + 256] = made.reshape(2, width // n_seq, 256)
+            to_core("q", 6, r.qc.at[1 - c], r.qcr)
+        else:
+            product(QUERY)
+            start(QUERY, 0)
+
+    def sums_product():
+        for j in range(0, 2 * width, 256):
+            if j < width:
+                made = dot_tn(r.q[:, j : j + 256], code_high)
+            else:
+                made = dot_tn(r.da[:, j - width : j - width + 256], value_code_low)
+            riding = pltpu.roll(r.vec[:, j // 2 : j // 2 + LANES].T, ONE + 1, 1).reshape(-1, rows, LANES)
+            made = made.reshape(-1, 2 * rows, LANES)
+            made = jnp.concatenate([made[:, :rows] + riding, made[:, rows:]], axis=1)
+            r.zc[heap * (j // 256) : heap * (j // 256 + 1)] = made.astype(BF16).reshape(heap, parts["c"], 2 * rows, LANES)
+        to_core("z", 8, r.zc.at[:, part("c", 1 - c)], r.zcr)
+
+    def query_line():
+        if apart:
+            core_copies.pop("q").wait()
+            r.qcr[...] = (r.qc[c].astype(F32) + r.qcr[...].astype(F32)).astype(BF16)
+            kept.sum_copies = exchange(
+                n_batch, z, on_z, lambda target: r.qcr.at[:, span_of(target, tall)], lambda slot: r.qz.at[slot], r.qz_s, r.qz_r
+            )
+
+    def down_product():
+        wait_all(cot_copies)
+        wait_all(act_copies)
+        for j in range(0, width, 256):
+            made = dot_tn(r.az[...], r.gz[:, j : j + 256]).astype(BF16)
+            r.dc[:, :, :, :, j : j + 256] = made.reshape(parts["a"], parts["b"], parts["c"], rows, 256)
+        to_core("d", 7, r.dc.at[:, :, part("c", 1 - c)], r.dcr)
+
+    def pixel_norm():
+        in_gain, in_shift = jnp.zeros((feat, 1), F32), jnp.zeros((feat, 1), F32)
+        for j in range(0, 2 * width, 256):
+            sums = r.zc[heap * (j // 256) : heap * (j // 256 + 1)].reshape(256, LANES)
+            spread = dot_nt(r.fct[...], jnp.concatenate([sums, sums], axis=1))
+            factor = r.kvw[:, j : j + 256].astype(F32)
+            in_gain = in_gain + jnp.sum(factor * spread[:feat], axis=1, keepdims=True)
+            in_shift = in_shift + jnp.sum(factor * spread[wide : wide + 1], axis=1, keepdims=True)
+        for at, column in ((0, in_gain), (1, in_shift)):
+            for j in range(0, feat, LANES):
+                some = min(LANES, feat - j)
+                eye = lax.broadcasted_iota(jnp.int32, (some, LANES), 0) == lax.broadcasted_iota(jnp.int32, (some, LANES), 1)
+                r.ar[0, at : at + 1, j : j + LANES] = jnp.sum(jnp.where(eye, column[j : j + some], 0.0), axis=0, keepdims=True)
+        kept.seq_copies = []
+        for offset in range(1, n_seq):
+            slot = n_seq - offset - 1
+            copy = pltpu.make_async_remote_copy(
+                src_ref=r.ar.at[0], dst_ref=r.ars.at[slot], send_sem=r.as_s.at[offset - 1], recv_sem=r.as_r.at[slot],
+                device_id=(z, lax.rem(s + offset, n_seq)), device_id_type=MESH,
+            )
+            copy.start()
+            kept.seq_copies.append(copy)
+
+    def sums_start():
+        core_copies.pop("z").wait()
+        both = r.zc[:, part("c", c)].astype(F32) + r.zcr[...].astype(F32)
+        r.zs0[0] = both.astype(BF16).reshape(parts["z"], parts["a"], parts["b"], 2 * rows, LANES)
+        start(SUMS, 0)
+
+    def down_start():
+        core_copies.pop("d").wait()
+        r.ds0[0, 0] = (r.dc[:, :, part("c", c)].astype(F32) + r.dcr[...].astype(F32)).astype(BF16)
+        start(DOWN, 0)
+
+    def pixel_gradient():
+        query_t, back_t = query_code.T, back_code.T
+        lifted = jnp.concatenate(
+            [
+                jnp.concatenate([pick_t * code_t[COLOR + channel : COLOR + channel + 1, :] for code_t in (query_t, back_t)], axis=1)
+                for channel in range(3)
+            ],
+            axis=0,
+        ).astype(BF16)
+        along = dot_nn(pick_t.astype(BF16), r.ye[...])
+        inv = r.ri[...]
+        cube = inv * inv * inv * along
+        colors = [r.xi[channel].astype(F32) for channel in range(3)]
+        for channel in range(3):
+            steep = dot_nn(lifted[channel * img : (channel + 1) * img], r.dp[...])
+            own_grad = inv * steep - cube * gram_row(channel, colors)[1]
+            window = jnp.concatenate([own_grad, jnp.zeros((img, LANES), F32)], axis=1)
+            for bit in range(7):
+                hop = 1 << bit
+                moved = pltpu.roll(window, hop, 1)
+                window = jnp.where((shift_of & hop) != 0, moved, window)
+            for j in range(9):
+                r.pg[j * img : (j + 1) * img, :] = window[:, j * LANES : (j + 1) * LANES]
+            grad_high, grad_low = split(r.pg[...])
+            r.pgs[channel] = dot_tn(r.sel[...], grad_high) + dot_tn(r.sel[...], grad_low)
+
+    def pixel_send():
+        kept.grad_copies = []
+        for offset in range(1, n_seq):
+            target = lax.rem(s + offset, n_seq)
+            copy = pltpu.make_async_remote_copy(
+                src_ref=r.pgs.at[:, pl.ds(pl.multiple_of(target * blocks, blocks), blocks), :],
+                dst_ref=r.pgr.at[n_seq - offset - 1],
+                send_sem=r.pg_s.at[offset - 1], recv_sem=r.pg_r.at[n_seq - offset - 1],
+                device_id=(z, target), device_id_type=MESH,
+            )
+            copy.start()
+            kept.grad_copies.append(copy)
+
+    def query_last():
+        if apart:
+            wait_all(kept.sum_copies)
+            made = gathered(r.qcr[:, span_of(z, tall)], r.qz, n_batch)
+            for j in range(0, tall, LANES):
+                r.qt[j : j + LANES, :] = made[:, j : j + LANES].T
+            few = tall // n_seq
+            part_q = r.qo.at[:, span_of(s, LANES)]
+            kept.last_copies = exchange(
+                n_seq, s, in_row, lambda target: r.qt.at[span_of(target, few), :], lambda slot: part_q, r.qo_s, r.qo_r
+            )
+            r.qo[:, span_of(s, LANES)] = r.qt[span_of(s, few), :]
+
+    def pixel_norm_line():
+        wait_all(kept.seq_copies)
+        r.ar[1] = gathered(r.ar[0], r.ars, n_seq)
+        kept.z_copies = exchange(n_batch, z, on_z, lambda target: r.ar.at[1], lambda slot: r.arz.at[slot], r.ab_s, r.ab_r)
+
     product(OUT)
     start(OUT, 0)
+    latents_gradient()
+    sums_product()
     step(UP, 0)
-
-    for j in range(0, width, 256):
-        r.ag[:, j : j + 256] = dot_nt(r.bt[QUERY, mine, :], r.wq[j : j + 256, :])
-
-    def latents_back(i, carry):
-        at = pl.ds(pl.multiple_of(i * tile, tile), tile)
-        grad, hat = r.ag[at, :], r.xl[at, :]
-        r.res[at, :] = r.res[at, :] + norm_back(grad, hat, r.rl[at, :1], qgain[...])
-        return carry[0] + jnp.sum(grad * hat, axis=0, keepdims=True), carry[1] + jnp.sum(grad, axis=0, keepdims=True)
-
-    gain_sum, shift_sum = lax.fori_loop(0, LANES // tile, latents_back, (zero, zero))
-    r.vec[0:1, :] = gain_sum
-    r.vec[1:2, :] = shift_sum
-    leave(r.res, o_lat.at[0])
-    if apart:
-        wait_all(norm_copies)
-        wait_all(query_copies)
-        for j in range(0, width, 256):
-            made = dot_tn(r.qp[...], r.np[:, j : j + 256]).astype(BF16)
-            r.qc[:, :, j : j + 256] = made.reshape(2, width // n_seq, 256)
-        to_core("q", 6, r.qc.at[1 - c], r.qcr)
-    else:
-        product(QUERY)
-        start(QUERY, 0)
-
-    heap = 256 // (2 * rows * parts["c"])
-    for j in range(0, 2 * width, 256):
-        if j < width:
-            made = dot_tn(r.q[:, j : j + 256], code_high)
-        else:
-            made = dot_tn(r.da[:, j - width : j - width + 256], value_code_low)
-        riding = pltpu.roll(r.vec[:, j // 2 : j // 2 + LANES].T, ONE + 1, 1).reshape(-1, rows, LANES)
-        made = made.reshape(-1, 2 * rows, LANES)
-        made = jnp.concatenate([made[:, :rows] + riding, made[:, rows:]], axis=1)
-        r.zc[heap * (j // 256) : heap * (j // 256 + 1)] = made.astype(BF16).reshape(heap, parts["c"], 2 * rows, LANES)
-    to_core("z", 8, r.zc.at[:, part("c", 1 - c)], r.zcr)
-    if apart:
-        core_copies.pop("q").wait()
-        r.qcr[...] = (r.qc[c].astype(F32) + r.qcr[...].astype(F32)).astype(BF16)
-        sum_copies = exchange(
-            n_batch, z, on_z, lambda target: r.qcr.at[:, span_of(target, tall)], lambda slot: r.qz.at[slot], r.qz_s, r.qz_r
-        )
-    wait_all(cot_copies)
-    wait_all(act_copies)
-    for j in range(0, width, 256):
-        made = dot_tn(r.az[...], r.gz[:, j : j + 256]).astype(BF16)
-        r.dc[:, :, :, :, j : j + 256] = made.reshape(parts["a"], parts["b"], parts["c"], rows, 256)
-    to_core("d", 7, r.dc.at[:, :, part("c", 1 - c)], r.dcr)
-
-    in_gain, in_shift = jnp.zeros((feat, 1), F32), jnp.zeros((feat, 1), F32)
-    for j in range(0, 2 * width, 256):
-        sums = r.zc[heap * (j // 256) : heap * (j // 256 + 1)].reshape(256, LANES)
-        spread = dot_nt(r.fct[...], jnp.concatenate([sums, sums], axis=1))
-        factor = r.kvw[:, j : j + 256].astype(F32)
-        in_gain = in_gain + jnp.sum(factor * spread[:feat], axis=1, keepdims=True)
-        in_shift = in_shift + jnp.sum(factor * spread[wide : wide + 1], axis=1, keepdims=True)
-    for at, column in ((0, in_gain), (1, in_shift)):
-        for j in range(0, feat, LANES):
-            some = min(LANES, feat - j)
-            eye = lax.broadcasted_iota(jnp.int32, (some, LANES), 0) == lax.broadcasted_iota(jnp.int32, (some, LANES), 1)
-            r.ar[0, at : at + 1, j : j + LANES] = jnp.sum(jnp.where(eye, column[j : j + some], 0.0), axis=0, keepdims=True)
-    seq_copies = []
-    for offset in range(1, n_seq):
-        slot = n_seq - offset - 1
-        copy = pltpu.make_async_remote_copy(
-            src_ref=r.ar.at[0], dst_ref=r.ars.at[slot], send_sem=r.as_s.at[offset - 1], recv_sem=r.as_r.at[slot],
-            device_id=(z, lax.rem(s + offset, n_seq)), device_id_type=MESH,
-        )
-        copy.start()
-        seq_copies.append(copy)
-    core_copies.pop("z").wait()
-    both = r.zc[:, part("c", c)].astype(F32) + r.zcr[...].astype(F32)
-    r.zs0[0] = both.astype(BF16).reshape(parts["z"], parts["a"], parts["b"], 2 * rows, LANES)
-    start(SUMS, 0)
-    core_copies.pop("d").wait()
-    r.ds0[0, 0] = (r.dc[:, :, part("c", c)].astype(F32) + r.dcr[...].astype(F32)).astype(BF16)
-    start(DOWN, 0)
-
-    query_t, back_t = query_code.T, back_code.T
-    lifted = jnp.concatenate(
-        [
-            jnp.concatenate([pick_t * code_t[COLOR + channel : COLOR + channel + 1, :] for code_t in (query_t, back_t)], axis=1)
-            for channel in range(3)
-        ],
-        axis=0,
-    ).astype(BF16)
-    along = dot_nn(pick_t.astype(BF16), r.ye[...])
-    inv = r.ri[...]
-    cube = inv * inv * inv * along
-    colors = [r.xi[channel].astype(F32) for channel in range(3)]
-    for channel in range(3):
-        steep = dot_nn(lifted[channel * img : (channel + 1) * img], r.dp[...])
-        own_grad = inv * steep - cube * gram_row(channel, colors)[1]
-        window = jnp.concatenate([own_grad, jnp.zeros((img, LANES), F32)], axis=1)
-        for bit in range(7):
-            hop = 1 << bit
-            moved = pltpu.roll(window, hop, 1)
-            window = jnp.where((shift_of & hop) != 0, moved, window)
-        for j in range(9):
-            r.pg[j * img : (j + 1) * img, :] = window[:, j * LANES : (j + 1) * LANES]
-        grad_high, grad_low = split(r.pg[...])
-        r.pgs[channel] = dot_tn(r.sel[...], grad_high) + dot_tn(r.sel[...], grad_low)
-    grad_copies = []
-    for offset in range(1, n_seq):
-        target = lax.rem(s + offset, n_seq)
-        copy = pltpu.make_async_remote_copy(
-            src_ref=r.pgs.at[:, pl.ds(pl.multiple_of(target * blocks, blocks), blocks), :],
-            dst_ref=r.pgr.at[n_seq - offset - 1],
-            send_sem=r.pg_s.at[offset - 1], recv_sem=r.pg_r.at[n_seq - offset - 1],
-            device_id=(z, target), device_id_type=MESH,
-        )
-        copy.start()
-        grad_copies.append(copy)
-
+    query_product()
+    pixel_norm()
+    query_line()
+    sums_start()
+    pixel_gradient()
+    step(OUT, 0)
     step(UP, 1)
-    if apart:
-        wait_all(sum_copies)
-        made = gathered(r.qcr[:, span_of(z, tall)], r.qz, n_batch)
-        for j in range(0, tall, LANES):
-            r.qt[j : j + LANES, :] = made[:, j : j + LANES].T
-        few = tall // n_seq
-        part_q = r.qo.at[:, span_of(s, LANES)]
-        last_copies = exchange(
-            n_seq, s, in_row, lambda target: r.qt.at[span_of(target, few), :], lambda slot: part_q, r.qo_s, r.qo_r
-        )
-        r.qo[:, span_of(s, LANES)] = r.qt[span_of(s, few), :]
-    else:
-        step(QUERY, 0)
-    step(OUT, 0)
+    pixel_send()
+    pixel_norm_line()
     step(SUMS, 0)
-    step(DOWN, 0)
-    wait_all(seq_copies)
-    r.ar[1] = gathered(r.ar[0], r.ars, n_seq)
-    z_copies = exchange(n_batch, z, on_z, lambda target: r.ar.at[1], lambda slot: r.arz.at[slot], r.ab_s, r.ab_r)
+    down_product()
+    query_last()
+    down_start()
     step(OUT, 1)
     step(SUMS, 1)
+    step(DOWN, 0)
     if not apart:
+        step(QUERY, 0)
         step(QUERY, 1)
 
     total_rows = width // (n_batch * n_seq)
@@ -800,17 +832,17 @@
             r.out[mat] = pltpu.roll(r.out[mat], lax.rem(rows - inner * total_rows, rows), 0)
         leave(r.out.at[mat, :total_rows], made)
 
-    wait_all(grad_copies)
+    wait_all(kept.grad_copies)
     o_pix[...] = gathered(r.pgs[:, own, :], r.pgr, n_seq)
-    finish(DOWN, o_wd)
     finish(UP, o_wu)
     if apart:
-        wait_all(last_copies)
+        wait_all(kept.last_copies)
         leave(r.qo, o_wq)
     else:
         finish(QUERY, o_wq)
-    wait_all(z_copies)
+    wait_all(kept.z_copies)
     o_in[...] = gathered(r.ar[1], r.arz, n_batch)[:, :feat]
+    finish(DOWN, o_wd)
     finish(OUT, o_wo)
     step(SUMS, 2)
     sums = r.zout[...]

time: 67.3 us -> 62.2 us (0.924)
  Pallas kernels: 66.3 us -> 61.2 us
    pallas_call x1, Pallas kernels: 63.8 us -> 58.7 us  [body(): pl.pallas_call(functools.partial(layer, n_batch, n_seq, width, n_img, fea...]
where the time goes in v4:
time: 62.2 us; the launch traced here: 62 us
  Pallas kernels  61.2 us (98%)
  between operations  0.82 us (1%)
    pallas_call x1, Pallas kernels, body(): pl.pallas_call(functools.partial(layer, n_batch, n_seq, width, n_img, fea...  58.7 us
    pallas_call x1, Pallas kernels, body(): pl.pallas_call(hand_over, out_shape=out_shape, in_specs=[vm] * len(made),...  2.46 us

profile of v4, /device:TPU:0, one launch (start us, length us, event | category | flops | bytes accessed | tf_op | source)
XLA Modules:
  0.0 62.0 jit_solution(15577247630235772105)
XLA Ops:
  0.7 58.7 %layer.1 = (bf16[1,128,1024]{2,1,0:T(8,128)(2,1)}, f32[1,128,1024]{2,1,0:T(8,128)}, f32[3,16,128]{2,1,0:T(8,128)}, f32[8,32]{1,0:T(8,128)}, f32[32,1024]{1,0:T(8...) custom-call(bf16[1,128,1024]{2,1,0:T(8,128)(2,1)} %h_lat.1, ...), custom_call_target="tpu_custom_call" | custom-call | tf_op jit(solution)/shard_map/layer/pallas_call | solution.py:900
  59.4 2.5 %hand_over.1 = (bf16[1,128,1024]{2,1,0:T(8,128)(2,1)}, f32[1,128,1024]{2,1,0:T(8,128)}, f32[3,1,2048]{2,1,0:T(1,128)}, f32[32]{0:T(128)}, f32[32]{0:T(128)}, /*i...) custom-call(bf16[1,128,1024]{2,1,0:T(8,128)(2,1)} %get-tuple-element, ...), custom_call_target="tpu_custom_call" | custom-call | tf_op jit(solution)/shard_map/hand_over/pallas_call | solution.py:917

commit v5 on v4

--- a/solution.py
+++ b/solution.py
@@ -306,6 +306,16 @@
             return pl.ds(half * rows, rows), slice(None)
         return slice(None), pl.ds(half * (width // 2), width // 2)
 
+    def renew(values):
+        flat = values.reshape(-1, LANES)
+        at = lax.broadcasted_iota(jnp.int32, flat.shape, 1)
+        joined = flat + pltpu.roll(flat, LANES - 4, 1)
+        high = joined.astype(BF16).astype(F32)
+        rest = pltpu.roll(joined - high, 4, 1)
+        riders = (at > ONE) & (at <= ONE + 4)
+        flat = jnp.where(riders, high, jnp.where((at > ONE + 4) & (at <= ONE + 8), rest, flat))
+        return flat.reshape(values.shape)
+
     def blocks_at(mat, half, stage, target=None):
         s0, received, i = buffers_of(mat)
         at = {"z": slice(None), "a": slice(None), "b": slice(None)}
@@ -334,7 +344,7 @@
             keep = blocks_at(mat, half, stage)
             total = gathered(s0[keep], received[half][stage].at[i], sizes[name])
             if stage < last:
-                s0[keep] = total.astype(BF16)
+                s0[keep] = (renew(total) if mat == SUMS else total).astype(BF16)
             elif mat == SUMS:
                 r.zout[cut(mat, half)] = total
             else:
@@ -685,7 +695,7 @@
             riding = pltpu.roll(r.vec[:, j // 2 : j // 2 + LANES].T, ONE + 1, 1).reshape(-1, rows, LANES)
             made = made.reshape(-1, 2 * rows, LANES)
             made = jnp.concatenate([made[:, :rows] + riding, made[:, rows:]], axis=1)
-            r.zc[heap * (j // 256) : heap * (j // 256 + 1)] = made.astype(BF16).reshape(heap, parts["c"], 2 * rows, LANES)
+            r.zc[heap * (j // 256) : heap * (j // 256 + 1)] = renew(made).astype(BF16).reshape(heap, parts["c"], 2 * rows, LANES)
         to_core("z", 8, r.zc.at[:, part("c", 1 - c)], r.zcr)
 
     def query_line():
@@ -730,7 +740,7 @@
     def sums_start():
         core_copies.pop("z").wait()
         both = r.zc[:, part("c", c)].astype(F32) + r.zcr[...].astype(F32)
-        r.zs0[0] = both.astype(BF16).reshape(parts["z"], parts["a"], parts["b"], 2 * rows, LANES)
+        r.zs0[0] = renew(both).astype(BF16).reshape(parts["z"], parts["a"], parts["b"], 2 * rows, LANES)
         start(SUMS, 0)
 
     def down_start():
@@ -855,6 +865,7 @@
     spread_left = jnp.concatenate([code_high, code_high, code_low], axis=1)
     o_kv[...] = dot_nt(jnp.concatenate([high, low, high], axis=1), spread_left)[: 2 * total_rows, :feat]
     square = jnp.concatenate([turned, jnp.zeros((LANES - 2 * rows, LANES), F32)], axis=0)
+    square = square + pltpu.roll(square, LANES - 4, 1)
     o_vec[...] = square.T[COLOR : COLOR + 8, :total_rows]
     wait_all(leaving)
 

time: 62.2 us -> 62.2 us (level)
  no operation moved by 1% of the time
where the time goes in v5:
time: 62.2 us; the launch traced here: 62 us
  Pallas kernels  61.1 us (98%)
  between operations  0.82 us (1%)
    pallas_call x1, Pallas kernels, body(): pl.pallas_call(functools.partial(layer, n_batch, n_seq, width, n_img, fea...  58.7 us
    pallas_call x1, Pallas kernels, body(): pl.pallas_call(hand_over, out_shape=out_shape, in_specs=[vm] * len(made),...  2.46 us

profile of v5, /device:TPU:0, one launch (start us, length us, event | category | flops | bytes accessed | tf_op | source)
XLA Modules:
  0.0 62.0 jit_solution(16130828394405158467)
XLA Ops:
  0.7 58.7 %layer.1 = (bf16[1,128,1024]{2,1,0:T(8,128)(2,1)}, f32[1,128,1024]{2,1,0:T(8,128)}, f32[3,16,128]{2,1,0:T(8,128)}, f32[8,32]{1,0:T(8,128)}, f32[32,1024]{1,0:T(8...) custom-call(bf16[1,128,1024]{2,1,0:T(8,128)(2,1)} %h_lat.1, ...), custom_call_target="tpu_custom_call" | custom-call | tf_op jit(solution)/shard_map/layer/pallas_call | solution.py:911
  59.3 2.5 %hand_over.1 = (bf16[1,128,1024]{2,1,0:T(8,128)(2,1)}, f32[1,128,1024]{2,1,0:T(8,128)}, f32[3,1,2048]{2,1,0:T(1,128)}, f32[32]{0:T(128)}, f32[32]{0:T(128)}, /*i...) custom-call(bf16[1,128,1024]{2,1,0:T(8,128)(2,1)} %get-tuple-element, ...), custom_call_target="tpu_custom_call" | custom-call | tf_op jit(solution)/shard_map/hand_over/pallas_call | solution.py:928

commit v6 on v5

--- a/solution.py
+++ b/solution.py
@@ -325,9 +325,9 @@
         at[path[stage]] = part(path[stage], here[path[stage]]) if target is None else target
         return (i, at["z"], at["a"], at["b"]) + cut(mat, half)
 
-    def start(mat, stage):
+    def start(mat, stage, halves=(0, 1)):
         s0, received, i = buffers_of(mat)
-        for half in range(2):
+        for half in halves:
             name = (orders[half] + ("z",))[stage]
             flying[mat, half] = start_stage(
                 (mat, half), stage, name,
@@ -349,8 +349,8 @@
                 r.zout[cut(mat, half)] = total
             else:
                 r.out[(mat,) + cut(mat, half)] = total[0] if mat == DOWN else total
-        if stage < last:
-            start(mat, stage + 1)
+            if stage < last:
+                start(mat, stage + 1, (half,))
 
     def exchange(n, index, device_at, src_of, dst, sends, receives):
         copies = []
@@ -811,8 +811,8 @@
     sums_product()
     step(UP, 0)
     query_product()
+    query_line()
     pixel_norm()
-    query_line()
     sums_start()
     pixel_gradient()
     step(OUT, 0)

time: 62.2 us -> 62.2 us (level)
  no operation moved by 1% of the time
where the time goes in v6:
time: 62.2 us; the launch traced here: 62 us
  Pallas kernels  61.1 us (98%)
  between operations  0.82 us (1%)
    pallas_call x1, Pallas kernels, body(): pl.pallas_call(functools.partial(layer, n_batch, n_seq, width, n_img, fea...  58.7 us
    pallas_call x1, Pallas kernels, body(): pl.pallas_call(hand_over, out_shape=out_shape, in_specs=[vm] * len(made),...  2.46 us

profile of v6, /device:TPU:0, one launch (start us, length us, event | category | flops | bytes accessed | tf_op | source)
XLA Modules:
  0.0 62.0 jit_solution(3987121756958158942)
XLA Ops:
  0.7 58.7 %layer.1 = (bf16[1,128,1024]{2,1,0:T(8,128)(2,1)}, f32[1,128,1024]{2,1,0:T(8,128)}, f32[3,16,128]{2,1,0:T(8,128)}, f32[8,32]{1,0:T(8,128)}, f32[32,1024]{1,0:T(8...) custom-call(bf16[1,128,1024]{2,1,0:T(8,128)(2,1)} %h_lat.1, ...), custom_call_target="tpu_custom_call" | custom-call | tf_op jit(solution)/shard_map/layer/pallas_call | solution.py:911
  59.3 2.5 %hand_over.1 = (bf16[1,128,1024]{2,1,0:T(8,128)(2,1)}, f32[1,128,1024]{2,1,0:T(8,128)}, f32[3,1,2048]{2,1,0:T(1,128)}, f32[32]{0:T(128)}, f32[32]{0:T(128)}, /*i...) custom-call(bf16[1,128,1024]{2,1,0:T(8,128)(2,1)} %get-tuple-element, ...), custom_call_target="tpu_custom_call" | custom-call | tf_op jit(solution)/shard_map/hand_over/pallas_call | solution.py:928
